TPU v7x, 256 devices: a whole 4x4x8 slice. The times are simulated.
256 devices in a mesh: cluster: 8 (over x, z_lo), sub: 32 (over y, z_hi, core).
Axes of the slice: x: 4, y: 4, z: 8 (z_hi: 4, z_lo: 2; z = z_hi * 2 + z_lo), core: 2. Of those that a mesh axis runs over, the one named last changes fastest.
Arguments:
- load_terms: float32 [256, 128, 1536], P(('cluster', 'sub')), may hold values from -60 to 60
- dual_operator: bfloat16 [256, 1536, 1536], P(('cluster', 'sub')), may hold values from -2 to 16, as said below
- dirichlet: bfloat16 [256, 1536, 1536], P(('cluster', 'sub')), may hold values from -2 to 16, as said below
- corner_coupling: bfloat16 [256, 1536, 24], P(('cluster', 'sub')), may hold values from -0.25 to 0.25
- coarse_inverse: float32 [768, 768], P(('cluster', 'sub')), may hold values from -2 to 4, as said below
- face_map: int32 [256, 6, 256], P(('cluster', 'sub')), may hold values from 0 to 255, as said below
- face_live: int32 [256, 6], P(('cluster', 'sub')), may hold values from 0 to 1, as said below
- corner_ids: int32 [256, 8], P(('cluster', 'sub')), may hold values from 0 to 255, as said below
Outputs:
- multipliers: float32 [256, 128, 1536], P(('cluster', 'sub'))
- residual: float32 [256, 128, 1536], P(('cluster', 'sub'))
Inputs may be any that keep to these rules, and one draw needn't show every extreme that they name: face_map[d, f] is a permutation of the slots of a face; the maps of the two sides of a face pair are inverse to each other. `face_live`: equal on the two sides of a face pair. `corner_ids`: the eight corners of a subdomain are the lattice vertices (c + a, s + b + 4 * e) for a, b, e in 0 and 1, taken modulo 8 and 32; each vertex has one number and is shared by eight subdomains. `dual_operator`: each subdomain's matrix is symmetric and positive definite. `dirichlet`: each subdomain's matrix is symmetric and positive definite. `coarse_inverse`: symmetric and positive definite.
All inputs are finite; a program needn't handle non-finite values.
Results may differ from a plain program's by a relative error of at most 0.0099.
Values sent between devices are 32-bit elements; how exact they have to be, the bound alone decides.
A program may use at most 128 MiB of HBM per device.

v0:
```python
import jax
import jax.numpy as jnp
from jax import lax
from jax.sharding import Mesh
from jax.sharding import PartitionSpec as P

ITERS = 2
STRIDE = 4
CLUSTER = ("cluster_0", "cluster_1")
SUB = ("sub_0", "sub_1", "sub_2")
CLUSTER_SUB = ("cluster_0", "cluster_1", "sub_0", "sub_1", "sub_2")


def padded(block, sides, width):
    for axis, dim in sides:
        count = lax.axis_size(axis)
        forward = [(i, i + 1) for i in range(count - 1)]
        forward.append((count - 1, 0))
        backward = [(target, source) for source, target in forward]
        low = lax.ppermute(
            lax.slice_in_dim(block, block.shape[dim] - width, None, axis=dim), axis, forward
        )
        high = lax.ppermute(lax.slice_in_dim(block, 0, width, axis=dim), axis, backward)
        block = jnp.concatenate([low, block, high], axis=dim)
    return block


def passed_along(value, axis, steps):
    count = lax.axis_size(axis)
    pairs = [(source, (source + steps) % count) for source in range(count)]
    return lax.ppermute(value, axis, pairs)


def one_axis_at_a_time(shard, axes):
    for axis in axes:
        shard = lax.psum(shard, axis)
    return shard


def local(
    load_terms,
    dual_operator,
    dirichlet,
    corner_coupling,
    coarse_inverse,
    face_map,
    face_live,
    corner_ids,
):
    local_loads = load_terms[0]
    operator_local = dual_operator[0]
    precond_local = dirichlet[0]
    coupling = corner_coupling[0]
    slot_maps = face_map[0]
    live_faces = face_live[0].astype(jnp.float32)
    corners = corner_ids[0]
    load_count = local_loads.shape[0]
    dual_size = local_loads.shape[1]
    face_size = dual_size // 6
    coarse_size = coarse_inverse.shape[1]
    coarse_index = (3 * corners[:, None] + jnp.arange(3, dtype=jnp.int32)[None, :]).reshape(-1)
    spread = (coarse_index[:, None] == jnp.arange(coarse_size, dtype=jnp.int32)[None, :]).astype(
        jnp.float32
    )

    def assemble(local_sum):
        face_parts = local_sum.reshape(load_count, 6, face_size)
        slab_pair = padded(jnp.stack([face_parts[:, 0], face_parts[:, 1]]), ((CLUSTER, 0),), 1)
        row_pair = padded(jnp.stack([face_parts[:, 2], face_parts[:, 3]]), ((SUB, 0),), 1)
        column_pair = []
        for source_face, shift_step in ((5, STRIDE), (4, -STRIDE)):
            column_pair.append(passed_along(face_parts[:, source_face], SUB, shift_step))
        received = [
            slab_pair[0],
            slab_pair[3],
            row_pair[0],
            row_pair[3],
            column_pair[0],
            column_pair[1],
        ]
        pieces = []
        for face_index in range(6):
            permuted = jnp.take(received[face_index], slot_maps[face_index], axis=1)
            pieces.append((face_parts[:, face_index] + permuted) * live_faces[face_index])
        return jnp.concatenate(pieces, axis=1)

    full_inverse = lax.all_gather(coarse_inverse, CLUSTER_SUB, axis=0, tiled=True)

    def precond_with_product(vector):
        local_term = jnp.dot(
            vector.astype(jnp.bfloat16), precond_local, preferred_element_type=jnp.float32
        )
        precond = assemble(local_term)
        product = 0.5 * one_axis_at_a_time(jnp.sum(vector * precond, axis=1), CLUSTER_SUB)
        return (precond, product)

    right_side = assemble(local_loads)
    multipliers = jnp.zeros_like(right_side)
    residual = right_side
    precond, residual_dot = precond_with_product(residual)
    direction = precond
    for iteration in range(ITERS):
        rounded = direction.astype(jnp.bfloat16)
        direct = jnp.dot(rounded, operator_local, preferred_element_type=jnp.float32)
        corner_terms = jnp.dot(rounded, coupling, preferred_element_type=jnp.float32)
        coarse_local = jnp.dot(corner_terms, spread, precision=lax.Precision.HIGHEST)
        apply_coarse_load = lax.psum(coarse_local, CLUSTER_SUB)
        solution = jnp.dot(apply_coarse_load, full_inverse.T, precision=lax.Precision.HIGHEST)
        corner_values = jnp.dot(solution, spread.T, precision=lax.Precision.HIGHEST).astype(
            jnp.bfloat16
        )
        back = lax.dot_general(
            corner_values, coupling, (((1,), (1,)), ((), ())), preferred_element_type=jnp.float32
        )
        dual_image = assemble(direct + back)
        curvature = 0.5 * one_axis_at_a_time(jnp.sum(direction * dual_image, axis=1), CLUSTER_SUB)
        dual_image, curvature = (dual_image, curvature)
        step_size = residual_dot / curvature
        multipliers = multipliers + step_size[:, None] * direction
        residual = residual - step_size[:, None] * dual_image
        if iteration + 1 < ITERS:
            precond, residual_new = precond_with_product(residual)
            direction = precond + (residual_new / residual_dot)[:, None] * direction
            residual_dot = residual_new
    return (multipliers[None], residual[None])


def solution(mesh):
    torus = Mesh(
        mesh.devices.reshape(4, 2, 4, 4, 2), ("cluster_0", "cluster_1", "sub_0", "sub_1", "sub_2")
    )
    in_specs = (
        P(CLUSTER_SUB, None, None),
        P(CLUSTER_SUB, None, None),
        P(CLUSTER_SUB, None, None),
        P(CLUSTER_SUB, None, None),
        P(CLUSTER_SUB, None),
        P(CLUSTER_SUB, None, None),
        P(CLUSTER_SUB, None),
        P(CLUSTER_SUB, None),
    )
    out_specs = (P(CLUSTER_SUB, None, None), P(CLUSTER_SUB, None, None))
    return jax.shard_map(local, mesh=torus, in_specs=in_specs, out_specs=out_specs, check_vma=False)
```

profile of v0, /device:TPU:1, one launch (start us, length us, event | category | flops | bytes accessed | tf_op | source)
XLA Modules:
  0.0 1243.5 jit_solution(12883256505124649430)
XLA Ops:
  9.5 7.8 collective-permute-start.4
  28.1 6.7 copy.173
  49.1 5.9 collective-permute-start.11
  59.7 5.5 collective-permute-start.10
  68.8 5.3 collective-permute-done.10
  86.3 341.6 %all-gather.3.cloned.1.call-done = f32[256,3,768]{2,1,0:T(4,128)} async-done(((f32[1,3,768]{2,1,0:T(4,128)}), f32[256,3,768]{2,1,0:T(4,128)}) %all-gather.3.cloned.1.call-update) | async-done | bytes 2359312 | tf_op jit(solution)/shard_map/all_gather | solution.py:87
  431.1 251.5 %all-reduce.8.cloned.1.call-done = f32[128,768]{1,0:T(8,128)} async-done(((f32[128,768]{1,0:T(8,128)}), f32[128,768]{1,0:T(8,128)}) %all-reduce.8.cloned.1.call-update) | async-done | bytes 393232 | tf_op jit(solution)/shard_map/psum | solution.py:107
  708.8 5.8 collective-permute-start.17
  749.9 8.4 all-reduce.2
  758.3 4.1 all-reduce.4
  762.3 6.6 all-reduce.1
  768.9 12.2 all-reduce
  781.1 4.6 all-reduce.3
  785.8 4.3 fusion.4
  840.0 6.0 psum.165
  850.0 7.0 psum.167
  857.0 14.4 %psum.168 = f32[128]{0:T(128)S(1)} all-reduce(f32[128]{0:T(128)S(1)} %psum.167), channel_id=1, replica_groups=mesh['cluster_0'=4,'cluster_1'=2,'sub_0'=4,'sub_1'=4,'sub_2'=2] {'sub_1'}, use_global_device_ids=true, to_apply=%region_17.19 | all-reduce | flops 128 | bytes 1024 | tf_op jit(solution)/shard_map/psum | solution.py:36
  871.4 10.1 psum.169
  888.4 238.6 %all-reduce.10.cloned.1.call-done = f32[128,768]{1,0:T(8,128)} async-done(((f32[128,768]{1,0:T(8,128)}), f32[128,768]{1,0:T(8,128)}) %all-reduce.10.cloned.1.call-update) | async-done | bytes 393232 | tf_op jit(solution)/shard_map/psum | solution.py:107
  1181.0 8.3 psum.171
  1189.3 4.2 psum.172
  1193.5 6.6 psum.173
  1200.1 11.9 psum.174
  1212.1 8.6 psum.175
  (372 shorter events, 241.9 us)
Async XLA Ops:
  7.2 420.7 %all-gather.3.cloned.1.call-start = ((), (), s32[]{:S(2)}) async-start(), calls=%async_computation.2 | async-start | bytes 3158016 | tf_op jit(solution)/shard_map/all_gather | solution.py:87
  7.9 674.7 %all-reduce.8.cloned.1.call-start = ((), (), s32[]{:S(2)}) async-start(), calls=%async_computation | async-start | bytes 786432 | tf_op jit(solution)/shard_map/psum | solution.py:107
  9.5 15.3 %collective-permute-start.4 = (f32[128,256]{1,0:T(8,128)S(1)}, f32[128,256]{1,0:T(8,128)S(1)}, u32[]{:S(2)}, u32[]{:S(2)}) collective-permute-start(f32[128,256]{1,0:T(8,128)S(1)} %bitcast.570), channel_id=1, source_target_pairs={{0,4},{1,5},{2,6},{3,7},{4,8},{5,9},{6,10},{7,11},{8,12},{9,13},{1... | collective-permute-start | bytes 393224 | tf_op jit(solution)/shard_map/ppermute | solution.py:31
  17.5 18.9 %collective-permute-start.1 = (f32[1,128,256]{2,1,0:T(8,128)S(1)}, f32[1,128,256]{2,1,0:T(8,128)S(1)}, u32[]{:S(2)}, u32[]{:S(2)}) collective-permute-start(f32[1,128,256]{2,1,0:T(8,128)S(1)} %bitcast.575), channel_id=1, source_target_pairs={{32,0},{64,32},{96,64},{128,96},{160,128},{192,160},{224,192},{0,2... | collective-permute-start | bytes 393224 | tf_op jit(solution)/shard_map/ppermute | solution.py:23
  20.6 16.7 %collective-permute-start = (f32[1,128,256]{2,1,0:T(8,128)S(1)}, f32[1,128,256]{2,1,0:T(8,128)S(1)}, u32[]{:S(2)}, u32[]{:S(2)}) collective-permute-start(f32[1,128,256]{2,1,0:T(8,128)S(1)} %bitcast.574), channel_id=1, source_target_pairs={{0,32},{32,64},{64,96},{96,128},{128,160},{160,192},{192,224},{224... | collective-permute-start | bytes 393224 | tf_op jit(solution)/shard_map/ppermute | solution.py:20
  20.8 17.5 %collective-permute-start.3 = (f32[1,128,256]{2,1,0:T(8,128)S(1)}, f32[1,128,256]{2,1,0:T(8,128)S(1)}, u32[]{:S(2)}, u32[]{:S(2)}) collective-permute-start(f32[1,128,256]{2,1,0:T(8,128)S(1)} %bitcast.572), channel_id=1, source_target_pairs={{1,0},{2,1},{3,2},{4,3},{5,4},{6,5},{7,6},{8,7},{9,8},{10,9},{11,1... | collective-permute-start | bytes 393224 | tf_op jit(solution)/shard_map/ppermute | solution.py:23
  22.2 17.0 %collective-permute-start.2 = (f32[1,128,256]{2,1,0:T(8,128)S(1)}, f32[1,128,256]{2,1,0:T(8,128)S(1)}, u32[]{:S(2)}, u32[]{:S(2)}) collective-permute-start(f32[1,128,256]{2,1,0:T(8,128)S(1)} %bitcast.571), channel_id=1, source_target_pairs={{0,1},{1,2},{2,3},{3,4},{4,5},{5,6},{6,7},{7,8},{8,9},{9,10},{10,1... | collective-permute-start | bytes 393224 | tf_op jit(solution)/shard_map/ppermute | solution.py:20
  24.8 15.4 %collective-permute-start.5 = (f32[128,256]{1,0:T(8,128)S(1)}, f32[128,256]{1,0:T(8,128)S(1)}, u32[]{:S(2)}, u32[]{:S(2)}) collective-permute-start(f32[128,256]{1,0:T(8,128)S(1)} %bitcast.573), channel_id=1, source_target_pairs={{0,28},{1,29},{2,30},{3,31},{4,0},{5,1},{6,2},{7,3},{8,4},{9,5},{1... | collective-permute-start | bytes 393224 | tf_op jit(solution)/shard_map/ppermute | solution.py:31
  49.1 16.6 %collective-permute-start.11 = (f32[128,256]{1,0:T(8,128)S(1)}, f32[128,256]{1,0:T(8,128)S(1)}, u32[]{:S(2)}, u32[]{:S(2)}) collective-permute-start(f32[128,256]{1,0:T(8,128)S(1)} %get-tuple-element.33), channel_id=1, source_target_pairs={{0,28},{1,29},{2,30},{3,31},{4,0},{5,1},{6,2},{7,3},{8,4},{9,5},{1... | collective-permute-start | bytes 393224 | tf_op jit(solution)/shard_map/ppermute | solution.py:31
  82.2 1044.9 %all-reduce.10.cloned.1.call-start = ((), (), s32[]{:S(2)}) async-start(), calls=%async_computation.1 | async-start | bytes 786432 | tf_op jit(solution)/shard_map/psum | solution.py:107
  694.2 14.7 %collective-permute-start.16 = (f32[128,256]{1,0:T(8,128)S(1)}, f32[128,256]{1,0:T(8,128)}, u32[]{:S(2)}, u32[]{:S(2)}) collective-permute-start(f32[128,256]{1,0:T(8,128)S(1)} %bitcast.576), channel_id=1, source_target_pairs={{0,4},{1,5},{2,6},{3,7},{4,8},{5,9},{6,10},{7,11},{8,12},{9,13},{1... | collective-permute-start | bytes 393224 | tf_op jit(solution)/shard_map/ppermute | solution.py:31
  697.6 21.1 %collective-permute-start.13 = (f32[1,128,256]{2,1,0:T(8,128)}, f32[1,128,256]{2,1,0:T(8,128)}, u32[]{:S(2)}, u32[]{:S(2)}) collective-permute-start(f32[1,128,256]{2,1,0:T(8,128)} %bitcast.581), channel_id=1, source_target_pairs={{32,0},{64,32},{96,64},{128,96},{160,128},{192,160},{224,192},{0,2... | collective-permute-start | bytes 393224 | tf_op jit(solution)/shard_map/ppermute | solution.py:23
  701.2 21.5 %collective-permute-start.12 = (f32[1,128,256]{2,1,0:T(8,128)}, f32[1,128,256]{2,1,0:T(8,128)}, u32[]{:S(2)}, u32[]{:S(2)}) collective-permute-start(f32[1,128,256]{2,1,0:T(8,128)} %bitcast.580), channel_id=1, source_target_pairs={{0,32},{32,64},{64,96},{96,128},{128,160},{160,192},{192,224},{224... | collective-permute-start | bytes 393224 | tf_op jit(solution)/shard_map/ppermute | solution.py:20
  702.9 23.8 %collective-permute-start.15 = (f32[1,128,256]{2,1,0:T(8,128)}, f32[1,128,256]{2,1,0:T(8,128)}, u32[]{:S(2)}, u32[]{:S(2)}) collective-permute-start(f32[1,128,256]{2,1,0:T(8,128)} %bitcast.579), channel_id=1, source_target_pairs={{1,0},{2,1},{3,2},{4,3},{5,4},{6,5},{7,6},{8,7},{9,8},{10,9},{11,1... | collective-permute-start | bytes 393224 | tf_op jit(solution)/shard_map/ppermute | solution.py:23
  707.2 23.5 %collective-permute-start.14 = (f32[1,128,256]{2,1,0:T(8,128)}, f32[1,128,256]{2,1,0:T(8,128)}, u32[]{:S(2)}, u32[]{:S(2)}) collective-permute-start(f32[1,128,256]{2,1,0:T(8,128)} %bitcast.578), channel_id=1, source_target_pairs={{0,1},{1,2},{2,3},{3,4},{4,5},{5,6},{6,7},{7,8},{8,9},{9,10},{10,1... | collective-permute-start | bytes 393224 | tf_op jit(solution)/shard_map/ppermute | solution.py:20
  708.8 25.9 %collective-permute-start.17 = (f32[128,256]{1,0:T(8,128)}, f32[128,256]{1,0:T(8,128)}, u32[]{:S(2)}, u32[]{:S(2)}) collective-permute-start(f32[128,256]{1,0:T(8,128)} %bitcast.577), channel_id=1, source_target_pairs={{0,28},{1,29},{2,30},{3,31},{4,0},{5,1},{6,2},{7,3},{8,4},{9,5},{1... | collective-permute-start | bytes 393224 | tf_op jit(solution)/shard_map/ppermute | solution.py:31
  796.6 16.2 %collective-permute-start.21 = (f32[1,128,256]{2,1,0:T(8,128)}, f32[1,128,256]{2,1,0:T(8,128)}, u32[]{:S(2)}, u32[]{:S(2)}) collective-permute-start(f32[1,128,256]{2,1,0:T(8,128)} %get-tuple-element.23), channel_id=1, source_target_pairs={{1,0},{2,1},{3,2},{4,3},{5,4},{6,5},{7,6},{8,7},{9,8},{10,9},{11,1... | collective-permute-start | bytes 393224 | tf_op jit(solution)/shard_map/ppermute | solution.py:23
  797.5 19.3 %collective-permute-start.22 = (f32[128,256]{1,0:T(8,128)}, f32[128,256]{1,0:T(8,128)}, u32[]{:S(2)}, u32[]{:S(2)}) collective-permute-start(f32[128,256]{1,0:T(8,128)} %get-tuple-element.24), channel_id=1, source_target_pairs={{0,4},{1,5},{2,6},{3,7},{4,8},{5,9},{6,10},{7,11},{8,12},{9,13},{1... | collective-permute-start | bytes 393224 | tf_op jit(solution)/shard_map/ppermute | solution.py:31
  799.0 21.8 %collective-permute-start.20 = (f32[1,128,256]{2,1,0:T(8,128)}, f32[1,128,256]{2,1,0:T(8,128)}, u32[]{:S(2)}, u32[]{:S(2)}) collective-permute-start(f32[1,128,256]{2,1,0:T(8,128)} %get-tuple-element.25), channel_id=1, source_target_pairs={{0,1},{1,2},{2,3},{3,4},{4,5},{5,6},{6,7},{7,8},{8,9},{9,10},{10,1... | collective-permute-start | bytes 393224 | tf_op jit(solution)/shard_map/ppermute | solution.py:20
  802.0 22.8 %collective-permute-start.18 = (f32[1,128,256]{2,1,0:T(8,128)}, f32[1,128,256]{2,1,0:T(8,128)}, u32[]{:S(2)}, u32[]{:S(2)}) collective-permute-start(f32[1,128,256]{2,1,0:T(8,128)} %get-tuple-element.26), channel_id=1, source_target_pairs={{0,32},{32,64},{64,96},{96,128},{128,160},{160,192},{192,224},{224... | collective-permute-start | bytes 393224 | tf_op jit(solution)/shard_map/ppermute | solution.py:20
  1134.6 14.8 %collective-permute-start.25 = (f32[1,128,256]{2,1,0:T(8,128)S(1)}, f32[1,128,256]{2,1,0:T(8,128)S(1)}, u32[]{:S(2)}, u32[]{:S(2)}) collective-permute-start(f32[1,128,256]{2,1,0:T(8,128)S(1)} %bitcast.585), channel_id=1, source_target_pairs={{32,0},{64,32},{96,64},{128,96},{160,128},{192,160},{224,192},{0,2... | collective-permute-start | bytes 393224 | tf_op jit(solution)/shard_map/ppermute | solution.py:23
  1137.0 15.6 %collective-permute-start.27 = (f32[1,128,256]{2,1,0:T(8,128)S(1)}, f32[1,128,256]{2,1,0:T(8,128)S(1)}, u32[]{:S(2)}, u32[]{:S(2)}) collective-permute-start(f32[1,128,256]{2,1,0:T(8,128)S(1)} %bitcast.583), channel_id=1, source_target_pairs={{1,0},{2,1},{3,2},{4,3},{5,4},{6,5},{7,6},{8,7},{9,8},{10,9},{11,1... | collective-permute-start | bytes 393224 | tf_op jit(solution)/shard_map/ppermute | solution.py:23
  1140.5 16.9 %collective-permute-start.26 = (f32[1,128,256]{2,1,0:T(8,128)}, f32[1,128,256]{2,1,0:T(8,128)}, u32[]{:S(2)}, u32[]{:S(2)}) collective-permute-start(f32[1,128,256]{2,1,0:T(8,128)} %bitcast.121), channel_id=1, source_target_pairs={{0,1},{1,2},{2,3},{3,4},{4,5},{5,6},{6,7},{7,8},{8,9},{9,10},{10,1... | collective-permute-start | bytes 393224 | tf_op jit(solution)/shard_map/ppermute | solution.py:20
  1144.4 21.9 %collective-permute-start.29 = (f32[128,256]{1,0:T(8,128)}, f32[128,256]{1,0:T(8,128)}, u32[]{:S(2)}, u32[]{:S(2)}) collective-permute-start(f32[128,256]{1,0:T(8,128)} %bitcast.128), channel_id=1, source_target_pairs={{0,28},{1,29},{2,30},{3,31},{4,0},{5,1},{6,2},{7,3},{8,4},{9,5},{1... | collective-permute-start | bytes 393224 | tf_op jit(solution)/shard_map/ppermute | solution.py:31
  (65 other events, 1850.4 us)
Sparse Core Ops, SparseCore 0:
  9.9 417.9 all-gather.2
  434.0 248.6 all-reduce.7
  884.5 242.4 all-reduce.9
where the time goes:
time: 1250 us; the launch traced here: 1240 us
  waiting for transfers between devices  841 us (67%)
  blocking collectives  117 us (9%)
  local copies, waits for them, and re-layouts  108 us (9%)
  starting transfers between devices  67.4 us (5%)
  other arithmetic  64.6 us (5%)
  matrix products  30.4 us (2%)
  between operations  15.6 us (1%)
    psum x2, waiting for transfers between devices, local(): apply_coarse_load = lax.psum(coarse_local, CLUSTER_SUB)  490 us
    all_gather x1, waiting for transfers between devices, local(): lax.all_gather(coarse_inverse, CLUSTER_SUB, axis=0, tiled=True)  342 us
    psum x15, blocking collectives, one_axis_at_a_time(): shard = lax.psum(shard, axis)  117 us
    gather x60, local copies, waits for them, and re-layouts, assemble(): permuted = jnp.take(received[face_index], slot_maps[face_index], axis=1)  56 us
    unnamed x30, other arithmetic  47.1 us
    ppermute x10, starting transfers between devices, passed_along(): return lax.ppermute(value, axis, pairs)  39.8 us
    unnamed x133, local copies, waits for them, and re-layouts  27.2 us
  transfers between devices with their start and end apart: 33, of which 5 were waited for; matrix products, arithmetic and copies ran while one was open for 9% of the time, Pallas kernels for 0%

commit v1 on v0

v1 whole, which is shorter than its diff:
```python
import functools

import jax
import jax.numpy as jnp
from jax import lax
from jax.experimental import pallas as pl
from jax.experimental.pallas import tpu as pltpu
from jax.sharding import PartitionSpec as P

MESH = pl.DeviceIdType.MESH
F32 = jnp.float32
BF16 = jnp.bfloat16
ROWS = 128
FACE = 256
ORDER = 1536
HALF = 384
SEND_ORDER = (4, 5, 2, 3, 0, 1)
NT = (((1,), (1,)), ((), ()))


def iota(shape, dim):
    return lax.broadcasted_iota(jnp.int32, shape, dim)


def third(value):
    return (value * 171) >> 9


def kernel(
    load_hbm,
    oper_hbm,
    prec_hbm,
    coup_ref,
    kinv_ref,
    map_ref,
    live_ref,
    ids_ref,
    mult_out,
    res_out,
    oper,
    prec,
    loads,
    resid,
    direc,
    outgo,
    income,
    permute,
    own_bt,
    wide,
    pick,
    spread,
    bmsg,
    brecv,
    kown,
    kplane,
    ksel,
    lsend,
    lrecv,
    zsend,
    zrecv,
    csend,
    crecv,
    fsend,
    frecv,
    s1send,
    s1recv,
    s2send,
    s2recv,
    load_sem,
    oper_sem,
    face_send,
    face_recv,
    b_send,
    b_recv,
    fan_send,
    fan_recv,
):
    c = lax.axis_index("cluster")
    s = lax.axis_index("sub")
    x, z_lo = c // 2, c % 2
    y, z_hi, core = s // 8, (s // 2) % 4, s % 2
    z = z_hi * 2 + z_lo
    group = x * 4 + y
    plane = group * 2 + core
    column = z * 2 + core

    def at(px, py, pz, pcore):
        return (px * 2 + pz % 2, py * 8 + (pz // 2) * 2 + pcore)

    def plane_peer(q):
        return at(q // 8, (q // 2) % 4, z, q % 2)

    def z_peer(q):
        return at(x, y, q, core)

    def column_peer(q):
        return at(x, y, q // 2, q % 2)

    def group_peer(q):
        return at(q // 4, q % 4, z, core)

    neighbours = (
        ((c + 7) % 8, s),
        ((c + 1) % 8, s),
        (c, (s + 31) % 32),
        (c, (s + 1) % 32),
        (c, (s + 28) % 32),
        (c, (s + 4) % 32),
    )

    barrier = pltpu.get_barrier_semaphore()
    for peer in neighbours:
        pl.semaphore_signal(barrier, inc=1, device_id=peer, device_id_type=MESH)

    def greet(peer_of, count, me):
        def body(k, carry):
            peer = peer_of(lax.rem(me + k, count))
            pl.semaphore_signal(barrier, inc=1, device_id=peer, device_id_type=MESH)
            return carry

        lax.fori_loop(1, count, body, 0)

    greet(plane_peer, 32, plane)
    greet(column_peer, 16, column)

    load_copies = []
    for face in range(6):
        copy = pltpu.make_async_copy(
            load_hbm.at[:, pl.ds(face * FACE, FACE)], loads.at[face], load_sem.at[face]
        )
        copy.start()
        load_copies.append(copy)
    prec_copy = pltpu.make_async_copy(prec_hbm, prec, oper_sem.at[0])
    oper_copy = pltpu.make_async_copy(oper_hbm, oper, oper_sem.at[1])
    prec_copy.start()
    oper_copy.start()

    def face_copy(turn, face):
        return pltpu.make_async_remote_copy(
            src_ref=loads.at[face] if turn == 0 else outgo.at[turn - 1, face],
            dst_ref=income.at[turn, face ^ 1],
            send_sem=face_send.at[turn, face],
            recv_sem=face_recv.at[turn, face ^ 1],
            device_id=neighbours[face],
            device_id_type=MESH,
        )

    def face_arrived(turn, face):
        face_copy(turn, face ^ 1).wait_recv()

    def fan_out(slot, peer_of, count, me, source_of, dest):
        def body(k, carry):
            q = lax.rem(me + k, count)
            pltpu.make_async_remote_copy(
                src_ref=source_of(q),
                dst_ref=dest.at[me],
                send_sem=fan_send.at[slot],
                recv_sem=fan_recv.at[slot],
                device_id=peer_of(q),
                device_id_type=MESH,
            ).start()
            return carry

        lax.fori_loop(1, count, body, 0)

    def fan_wait(sem, slot, dest):
        part = dest.at[pl.ds(0, dest.shape[0] - 1)]
        pltpu.make_async_copy(part, part, sem.at[slot]).wait()

    pl.semaphore_wait(barrier, 6 + 31 + 15)

    for face in SEND_ORDER:
        load_copies[face].wait()
        face_copy(0, face).start()

    unit = (iota((32, 24), 0) == iota((32, 24), 1)).astype(F32).astype(BF16)
    turned = lax.dot_general(unit, coup_ref[...], NT, preferred_element_type=F32)
    row = iota((32, 128), 0)
    which = third(row)
    part = row - 3 * which
    natural = jnp.full((32, 128), -1, jnp.int32)
    placed = jnp.full((32, 128), -1, jnp.int32)
    for k in range(8):
        number = jnp.full((32, 128), ids_ref[0, k], jnp.int32)
        nc, ns = number >> 5, number & 31
        nz = (((ns >> 1) & 3) << 1) + (nc & 1)
        np_ = ((nc >> 1) << 3) + ((ns >> 3) << 1) + (ns & 1)
        hit = which == k
        natural = jnp.where(hit, 3 * number + part, natural)
        placed = jnp.where(hit, nz * 128 + 3 * np_ + part, placed)
    placed_f = placed.astype(F32)
    for face in range(6):
        bmsg[face, :, :FACE] = turned[:, face * FACE : (face + 1) * FACE]
        bmsg[face, :, FACE:] = placed_f
    b_copies = []
    for face in SEND_ORDER:
        copy = pltpu.make_async_remote_copy(
            src_ref=bmsg.at[face],
            dst_ref=brecv.at[face ^ 1],
            send_sem=b_send.at[face],
            recv_sem=b_recv.at[face ^ 1],
            device_id=neighbours[face],
            device_id_type=MESH,
        )
        copy.start()
        b_copies.append(copy)
    own_bt[...] = turned.astype(BF16)

    kown[...] = jnp.zeros_like(kown)
    kown[0, 0:3, :] = kinv_ref[:, :HALF]
    kown[1, 0:3, :] = kinv_ref[:, HALF:]
    fan_out(0, plane_peer, 32, plane, lambda q: kown.at[q % 2], kplane)
    kplane[plane] = kown[core]

    lanes768 = iota((32, 768), 1)
    spread[...] = (
        (jnp.concatenate([natural] * 6, axis=1) == lanes768).astype(F32).astype(BF16)
    )

    def build_permute(face, carry):
        target = jnp.broadcast_to(map_ref[face], (FACE, FACE))
        hot = (iota((FACE, FACE), 0) == target).astype(F32)
        alive = live_ref[0, face].astype(F32)
        permute[face] = (hot * alive).astype(BF16)
        return carry

    lax.fori_loop(0, 6, build_permute, 0)

    def clear(turn):
        outgo[turn] = jnp.zeros((6, ROWS, FACE), F32)

    def permuted(turn, face):
        value = income[turn, face]
        high = value.astype(BF16)
        low = (value - high.astype(F32)).astype(BF16)
        both = jnp.dot(
            jnp.concatenate([high, low], axis=0), permute[face], preferred_element_type=F32
        )
        return both[:ROWS] + both[ROWS:]

    def alive_of(face):
        return live_ref[0, face].astype(F32)

    def fold(value):
        return value[:, :128] + value[:, 128:]

    def multiply(turn, face, rounded, matrix, field):
        if face < 5:
            product = jnp.dot(rounded, matrix[face], preferred_element_type=F32)
            for n in range(6):
                outgo[turn, n] += product[:, n * FACE : (n + 1) * FACE]
            return None
        total = jnp.zeros((ROWS, 128), F32)
        for n in SEND_ORDER:
            value = outgo[turn, n] + jnp.dot(
                rounded, matrix[face, :, n * FACE : (n + 1) * FACE], preferred_element_type=F32
            )
            outgo[turn, n] = value
            face_copy(turn + 1, n).start()
            total = total + fold(field[n] * value)
        return total

    def lane_row(total):
        return jnp.sum(total.T, axis=0, keepdims=True)

    def spread_rows(line):
        wide_ = jnp.broadcast_to(line, (128, 128)).T
        return jnp.concatenate([wide_, wide_], axis=1)

    def scalars_start(turn, first, second):
        s1send[turn] = jnp.concatenate([first, second, jnp.zeros((6, 128), F32)], axis=0)
        fan_out(1 + turn, group_peer, 16, group, lambda q: s1send.at[turn], s1recv.at[turn])
        s1recv[turn, group] = s1send[turn]

    def scalars_middle(turn):
        fan_wait(fan_recv, 1 + turn, s1recv.at[turn])
        s2send[turn] = jnp.sum(s1recv[turn], axis=0)
        fan_out(4 + turn, column_peer, 16, column, lambda q: s2send.at[turn], s2recv.at[turn])
        s2recv[turn, column] = s2send[turn]

    def scalars_end(turn):
        fan_wait(fan_recv, 4 + turn, s2recv.at[turn])
        return jnp.sum(s2recv[turn], axis=0)

    def coarse_start(turn, terms):
        high = terms.astype(BF16)
        rest = terms - high.astype(F32)
        middle = rest.astype(BF16)
        low = (rest - middle.astype(F32)).astype(BF16)
        stacked = jnp.concatenate([high, middle, low], axis=0)
        full = jnp.dot(stacked, spread[...], preferred_element_type=F32)
        full = full[:ROWS] + full[ROWS : 2 * ROWS] + full[2 * ROWS :]
        for half in range(2):
            lsend[turn, half] = full[:, half * HALF : (half + 1) * HALF].reshape(16, 8, HALF)
        fan_out(
            7 + turn,
            plane_peer,
            32,
            plane,
            lambda q: lsend.at[turn, q % 2, q // 2],
            lrecv.at[turn],
        )
        lrecv[turn, plane] = lsend[turn, core, group]

    def coarse_sum(turn):
        fan_wait(fan_recv, 7 + turn, lrecv.at[turn])
        zsend[turn] = jnp.sum(lrecv[turn], axis=0)
        fan_out(9 + turn, z_peer, 8, z, lambda q: zsend.at[turn], zrecv.at[turn])
        zrecv[turn, z] = zsend[turn]

    def coarse_apply(turn):
        fan_wait(fan_recv, 9 + turn, zrecv.at[turn])
        load = jnp.sum(zrecv[turn], axis=0)
        csend[turn] = lax.dot_general(
            load,
            ksel[...],
            NT,
            precision=lax.Precision.HIGHEST,
            preferred_element_type=F32,
        )
        fan_out(11 + turn, column_peer, 16, column, lambda q: csend.at[turn], crecv.at[turn])
        crecv[turn, column] = csend[turn]

    def coarse_share(turn):
        fan_wait(fan_recv, 11 + turn, crecv.at[turn])
        energy = jnp.zeros((8, 128), F32)
        pieces = []
        for plane_z in range(8):
            both = crecv[turn, 2 * plane_z] + crecv[turn, 2 * plane_z + 1]
            pieces.append(both[:, :128])
            energy = energy + both[:, :128] * both[:, 128:]
        energy = jnp.sum(energy, axis=1, keepdims=True)
        pieces[0] = jnp.where(iota((8, 128), 1) == 96, energy, pieces[0])
        fsend[turn] = jnp.concatenate(pieces, axis=1)
        fan_out(13 + turn, group_peer, 16, group, lambda q: fsend.at[turn], frecv.at[turn])
        frecv[turn, group] = fsend[turn]

    def coarse_values(turn):
        fan_wait(fan_recv, 13 + turn, frecv.at[turn])
        field = frecv[turn].reshape(ROWS, 1024)
        values = lax.dot_general(
            field.astype(BF16), pick[...], NT, preferred_element_type=F32
        ).astype(BF16)
        energy = jnp.broadcast_to(field[:, 96:97], (ROWS, FACE))
        return values, energy

    clear(0)
    prec_copy.wait()
    for face in range(6):
        face_arrived(0, face)
        value = alive_of(face) * loads[face] + permuted(0, face)
        resid[face] = value
        dots = multiply(0, face, value.astype(BF16), prec, resid)
    first_rz = lane_row(dots)

    clear(1)
    wide[...] = jnp.zeros_like(wide)
    for face in range(6):
        wide[0:32, face * FACE : (face + 1) * FACE] = (
            bmsg[face, :, :FACE] * alive_of(face)
        ).astype(BF16)
    lane = iota((32, 1024), 1).astype(F32)
    pick[...] = jnp.zeros_like(pick)
    pick[0:32, :] = (
        (jnp.concatenate([placed_f] * 8, axis=1) == lane).astype(F32).astype(BF16)
    )
    for face in range(6):
        b_copies[SEND_ORDER.index(face ^ 1)].wait_recv()
        start = 32 * (face + 1)
        wide[start : start + 32, face * FACE : (face + 1) * FACE] = jnp.dot(
            brecv[face, :, :FACE].astype(BF16), permute[face], preferred_element_type=F32
        ).astype(BF16)
        place = brecv[face, :, FACE:]
        pick[start : start + 32, :] = (
            (jnp.concatenate([place] * 8, axis=1) == lane).astype(F32).astype(BF16)
        )
    fan_wait(fan_recv, 0, kplane)
    line = iota((128, 256), 0)
    packed = third(line)
    choose = jnp.where(
        line < 96, (iota((128, 256), 1) == packed * 8 + line - 3 * packed).astype(F32), 0.0
    )
    ksel[0:128, :] = jnp.dot(
        choose,
        kplane[...].reshape(256, HALF),
        precision=lax.Precision.HIGHEST,
        preferred_element_type=F32,
    )
    line = iota((128, HALF), 0)
    packed = third(line)
    owner = (
        ((packed >> 3) * 2 + z_lo) * 32 + ((packed >> 1) & 3) * 8 + z_hi * 2 + (packed & 1)
    )
    wanted = 3 * owner + line - 3 * packed
    ksel[128:256, :] = jnp.where(
        line < 96, (iota((128, HALF), 1) + HALF * core == wanted).astype(F32), 0.0
    )

    oper_copy.wait()
    rz = None
    for iteration in range(2):
        back = 2 * iteration + 1
        terms = jnp.zeros((ROWS, 32), F32)
        for face in range(6):
            face_arrived(back, face)
            value = alive_of(face) * outgo[back - 1, face] + permuted(back, face)
            if iteration == 1:
                if face == 0:
                    scalars_middle(1)
                    new_rz = scalars_end(1)[0:1]
                    beta = spread_rows(new_rz / rz)
                    rz = new_rz
                value = value + beta * direc[face]
            direc[face] = value
            rounded = value.astype(BF16)
            terms = terms + lax.dot_general(
                rounded,
                own_bt[:, face * FACE : (face + 1) * FACE],
                NT,
                preferred_element_type=F32,
            )
            dots = multiply(back, face, rounded, oper, direc)
        coarse_start(iteration, terms)
        scalars_start(2 * iteration, lane_row(dots), first_rz)
        coarse_sum(iteration)
        scalars_middle(2 * iteration)
        coarse_apply(iteration)
        totals = scalars_end(2 * iteration)
        if iteration == 0:
            rz = totals[1:2]
            clear(2)
        coarse_share(iteration)
        if iteration == 0:
            clear(3)
        values, energy = coarse_values(iteration)
        curvature = spread_rows(totals[0:1]) + energy
        step = spread_rows(rz) / curvature
        for face in range(6):
            face_arrived(back + 1, face)
            cols = slice(face * FACE, (face + 1) * FACE)
            image = (
                alive_of(face) * outgo[back, face]
                + permuted(back + 1, face)
                + jnp.dot(values, wide[:, cols], preferred_element_type=F32)
            )
            gain = step * direc[face]
            value = resid[face] - step * image
            if iteration == 0:
                mult_out[:, cols] = gain
                resid[face] = value
                dots = multiply(2, face, value.astype(BF16), prec, resid)
            else:
                mult_out[:, cols] += gain
                res_out[:, cols] = value
        if iteration == 0:
            scalars_start(1, lane_row(dots), first_rz)

    for turn in range(5):
        for face in range(6):
            face_copy(turn, face).wait_send()
    for copy in b_copies:
        copy.wait_send()
    fan_wait(fan_send, 0, kplane)
    for turn in range(3):
        fan_wait(fan_send, 1 + turn, s1recv.at[turn])
        fan_wait(fan_send, 4 + turn, s2recv.at[turn])
    for turn in range(2):
        fan_wait(fan_send, 7 + turn, lrecv.at[turn])
        fan_wait(fan_send, 9 + turn, zrecv.at[turn])
        fan_wait(fan_send, 11 + turn, crecv.at[turn])
        fan_wait(fan_send, 13 + turn, frecv.at[turn])


def local(load_terms, oper, prec, coupling, kinv, face_map, face_live, ids):
    any_ = pl.BlockSpec(memory_space=pl.ANY)
    vmem = pl.BlockSpec(memory_space=pltpu.VMEM)
    smem = pl.BlockSpec(memory_space=pltpu.SMEM)
    dma = pltpu.SemaphoreType.DMA

    def buf(*shape, dtype=F32):
        return pltpu.VMEM(shape, dtype)

    field = jax.ShapeDtypeStruct((ROWS, ORDER), F32)
    mult, res = pl.pallas_call(
        kernel,
        out_shape=(field, field),
        in_specs=[any_, any_, any_, vmem, vmem, vmem, smem, smem],
        out_specs=(vmem, vmem),
        scratch_shapes=[
            buf(6, FACE, ORDER, dtype=BF16),
            buf(6, FACE, ORDER, dtype=BF16),
            buf(6, ROWS, FACE),
            buf(6, ROWS, FACE),
            buf(6, ROWS, FACE),
            buf(4, 6, ROWS, FACE),
            buf(5, 6, ROWS, FACE),
            buf(6, FACE, FACE, dtype=BF16),
            buf(32, ORDER, dtype=BF16),
            buf(256, ORDER, dtype=BF16),
            buf(256, 1024, dtype=BF16),
            buf(32, 768, dtype=BF16),
            buf(6, 32, 384),
            buf(6, 32, 384),
            buf(2, 8, HALF),
            buf(32, 8, HALF),
            buf(256, HALF),
            buf(2, 2, 16, 8, HALF),
            buf(2, 32, 8, HALF),
            buf(2, 8, HALF),
            buf(2, 8, 8, HALF),
            buf(2, 8, 256),
            buf(2, 16, 8, 256),
            buf(2, 8, 1024),
            buf(2, 16, 8, 1024),
            buf(3, 8, 128),
            buf(3, 16, 8, 128),
            buf(3, 8, 128),
            buf(3, 16, 8, 128),
            dma((6,)),
            dma((2,)),
            dma((5, 6)),
            dma((5, 6)),
            dma((6,)),
            dma((6,)),
            dma((15,)),
            dma((15,)),
        ],
        compiler_params=pltpu.CompilerParams(
            collective_id=0, has_side_effects=True, vmem_limit_bytes=60 * 1024 * 1024
        ),
        cost_estimate=pl.CostEstimate(
            flops=2_600_000_000, bytes_accessed=12_000_000, transcendentals=0
        ),
        name="feti_solve",
    )(
        load_terms[0],
        oper.reshape(6, FACE, ORDER),
        prec.reshape(6, FACE, ORDER),
        coupling[0],
        kinv,
        face_map.reshape(6, 1, FACE),
        face_live,
        ids,
    )
    return mult[None], res[None]


def solution(mesh):
    both = ("cluster", "sub")
    wide = P(both, None, None)
    flat = P(both, None)
    return jax.shard_map(
        local,
        mesh=mesh,
        in_specs=(wide, wide, wide, wide, flat, wide, flat, flat),
        out_specs=(wide, wide),
        check_vma=False,
    )
```

time: 1250 us -> 188 us (0.15)
  waiting for transfers between devices: 841 us -> 0 us
  Pallas kernels: 0 us -> 181 us
  blocking collectives: 117 us -> 0 us
  local copies, waits for them, and re-layouts: 108 us -> 5.94 us
  starting transfers between devices: 67.4 us -> 0 us
  other arithmetic: 64.6 us -> 0 us
  matrix products: 30.4 us -> 0 us
  between operations: 15.6 us -> 0.64 us
    psum x2 -> x0, waiting for transfers between devices: 490 us -> none  [local(): apply_coarse_load = lax.psum(coarse_local, CLUSTER_SUB)]
    all_gather x1 -> x0, waiting for transfers between devices: 342 us -> none  [local(): lax.all_gather(coarse_inverse, CLUSTER_SUB, axis=0, tiled=True)]
    pallas_call x0 -> x1, Pallas kernels: none -> 181 us  [local(): pl.pallas_call(kernel, out_shape=(field, field), in_specs=[any_, any_, an...]
    psum x15 -> x0, blocking collectives: 117 us -> none  [one_axis_at_a_time(): shard = lax.psum(shard, axis)]
    ppermute x30 -> x0, starting transfers between devices: 67.3 us -> none  [the longest x10 39.8 us: passed_along(): return lax.ppermute(value, axis, pairs)]
    gather x60 -> x0, local copies, waits for them, and re-layouts: 56 us -> none  [assemble(): permuted = jnp.take(received[face_index], slot_maps[face_index], axis=1)]
    unnamed x30 -> x0, other arithmetic: 47.1 us -> none
    dot_general x14 -> x0, matrix products: 30.4 us -> none  [the longest x2 8.23 us: precond_with_product(): jnp.dot(vector.astype(jnp.bfloat16), precond_local, preferred_element_typ...]
  transfers between devices with their start and end apart: 33 -> 0, of which waited for: 5 -> 0; matrix products, arithmetic and copies ran while one was open for 9% -> 0% of each run, Pallas kernels for 0% -> 0%
where the time goes in v1:
time: 188 us
  Pallas kernels  181 us (96%)
  local copies, waits for them, and re-layouts  5.94 us (3%)
    pallas_call x1, Pallas kernels, local(): pl.pallas_call(kernel, out_shape=(field, field), in_specs=[any_, any_, an...  181 us
    unnamed x3, local copies, waits for them, and re-layouts  5.94 us

profile of v1, /device:TPU:1, one launch (start us, length us, event | category | flops | bytes accessed | tf_op | source)
XLA Modules:
  0.0 188.0 jit_solution(3102462608690971386)
XLA Ops:
  0.6 1.8 copy.10
  2.4 181.4 %feti_solve.1 = (f32[128,1536]{1,0:T(8,128)}, f32[128,1536]{1,0:T(8,128)}) custom-call(f32[128,1536]{1,0:T(8,128)} %bitcast.10, bf16[6,256,1536]{2,1,0:T(8,128)(2,1)} %bitcast.7, bf16[6,256,1536]{2,1,0:T(8,128)(2,1)} %bitcast.8, bf16[1536,24]{1,0:T(8,128)(2,1)} %bitcast.9, f32[3,768]{1,0:T(4,128)} %kinv_ref.1, s32[6,1,256]{2,1,0:T(1,128)} %bitcast.13, ...), custom_call_target="tpu_custom_call" | custom-call | flops 2600000000 | bytes 12000000 | tf_op jit(solution)/shard_map/feti_solve/pallas_call | solution.py:484
  183.8 2.1 %copy.13 = f32[1,128,1536]{2,1,0:T(8,128)} copy(f32[1,128,1536]{2,1,0:T(8,128)} %bitcast.12) | data formatting | bytes 1572864
  185.9 2.1 %copy.14 = f32[1,128,1536]{2,1,0:T(8,128)} copy(f32[1,128,1536]{2,1,0:T(8,128)} %bitcast.11) | data formatting | bytes 1572864

commit v2 on v1

--- a/solution.py
+++ b/solution.py
@@ -14,6 +14,7 @@
 FACE = 256
 ORDER = 1536
 HALF = 384
+PART = 64
 SEND_ORDER = (4, 5, 2, 3, 0, 1)
 NT = (((1,), (1,)), ((), ()))
 
@@ -45,15 +46,18 @@
     outgo,
     income,
     permute,
-    own_bt,
     wide,
     pick,
     spread,
+    values,
     bmsg,
     brecv,
     kown,
     kplane,
     ksel,
+    csave,
+    dots,
+    beta_rows,
     lsend,
     lrecv,
     zsend,
@@ -135,18 +139,23 @@
     prec_copy.start()
     oper_copy.start()
 
-    def face_copy(turn, face):
+    def rows_of(half):
+        return pl.ds(pl.multiple_of(half * PART, PART), PART)
+
+    def face_copy(turn, half, face):
+        rows = rows_of(half)
         return pltpu.make_async_remote_copy(
-            src_ref=loads.at[face] if turn == 0 else outgo.at[turn - 1, face],
-            dst_ref=income.at[turn, face ^ 1],
-            send_sem=face_send.at[turn, face],
-            recv_sem=face_recv.at[turn, face ^ 1],
+            src_ref=loads.at[face, rows] if turn == 0 else outgo.at[turn - 1, face, rows],
+            dst_ref=income.at[turn, face ^ 1, rows],
+            send_sem=face_send.at[turn, half, face],
+            recv_sem=face_recv.at[turn, half, face ^ 1],
             device_id=neighbours[face],
             device_id_type=MESH,
         )
 
-    def face_arrived(turn, face):
-        face_copy(turn, face ^ 1).wait_recv()
+    def face_wait(sem, turn, half, face):
+        part = income.at[turn, face, rows_of(half)]
+        pltpu.make_async_copy(part, part, sem.at[turn, half, face]).wait()
 
     def fan_out(slot, peer_of, count, me, source_of, dest):
         def body(k, carry):
@@ -169,29 +178,28 @@
 
     pl.semaphore_wait(barrier, 6 + 31 + 15)
 
-    for face in SEND_ORDER:
-        load_copies[face].wait()
-        face_copy(0, face).start()
-
-    unit = (iota((32, 24), 0) == iota((32, 24), 1)).astype(F32).astype(BF16)
-    turned = lax.dot_general(unit, coup_ref[...], NT, preferred_element_type=F32)
-    row = iota((32, 128), 0)
-    which = third(row)
-    part = row - 3 * which
-    natural = jnp.full((32, 128), -1, jnp.int32)
-    placed = jnp.full((32, 128), -1, jnp.int32)
+    for half in range(2):
+        for face in SEND_ORDER:
+            if half == 0:
+                load_copies[face].wait()
+            face_copy(0, half, face).start()
+
+    turned = coup_ref[...].astype(F32)
+    zero = jnp.zeros((8, FACE), F32)
+    corner = iota((8, 128), 0)
+    natural = jnp.zeros((8, 128), jnp.int32)
+    placed = jnp.zeros((8, 128), jnp.int32)
     for k in range(8):
-        number = jnp.full((32, 128), ids_ref[0, k], jnp.int32)
+        number = jnp.full((8, 128), ids_ref[0, k], jnp.int32)
         nc, ns = number >> 5, number & 31
         nz = (((ns >> 1) & 3) << 1) + (nc & 1)
         np_ = ((nc >> 1) << 3) + ((ns >> 3) << 1) + (ns & 1)
-        hit = which == k
-        natural = jnp.where(hit, 3 * number + part, natural)
-        placed = jnp.where(hit, nz * 128 + 3 * np_ + part, placed)
-    placed_f = placed.astype(F32)
+        natural = jnp.where(corner == k, 3 * number, natural)
+        placed = jnp.where(corner == k, nz * 128 + 3 * np_, placed)
+    places = jnp.concatenate([natural, placed], axis=1).astype(F32)
     for face in range(6):
-        bmsg[face, :, :FACE] = turned[:, face * FACE : (face + 1) * FACE]
-        bmsg[face, :, FACE:] = placed_f
+        bmsg[face, 0:24, :] = turned[:, face * FACE : (face + 1) * FACE]
+        bmsg[face, 24:32, :] = places
     b_copies = []
     for face in SEND_ORDER:
         copy = pltpu.make_async_remote_copy(
@@ -204,7 +212,6 @@
         )
         copy.start()
         b_copies.append(copy)
-    own_bt[...] = turned.astype(BF16)
 
     kown[...] = jnp.zeros_like(kown)
     kown[0, 0:3, :] = kinv_ref[:, :HALF]
@@ -212,56 +219,92 @@
     fan_out(0, plane_peer, 32, plane, lambda q: kown.at[q % 2], kplane)
     kplane[plane] = kown[core]
 
-    lanes768 = iota((32, 768), 1)
-    spread[...] = (
-        (jnp.concatenate([natural] * 6, axis=1) == lanes768).astype(F32).astype(BF16)
-    )
+    def alive_of(face):
+        return live_ref[0, face].astype(F32)
 
     def build_permute(face, carry):
         target = jnp.broadcast_to(map_ref[face], (FACE, FACE))
         hot = (iota((FACE, FACE), 0) == target).astype(F32)
-        alive = live_ref[0, face].astype(F32)
-        permute[face] = (hot * alive).astype(BF16)
+        permute[face] = (hot * alive_of(face)).astype(BF16)
         return carry
 
     lax.fori_loop(0, 6, build_permute, 0)
 
     def clear(turn):
-        outgo[turn] = jnp.zeros((6, ROWS, FACE), F32)
-
-    def permuted(turn, face):
-        value = income[turn, face]
+        def body(face, carry):
+            outgo[turn, face] = jnp.zeros((ROWS, FACE), F32)
+            return carry
+
+        lax.fori_loop(0, 6, body, 0)
+
+    row = iota((32, 128), 0)
+    which = third(row)
+    part = (row - 3 * which).astype(F32)
+
+    def one_hot(message):
+        first = jnp.full((32, 128), -4.0, F32)
+        second = jnp.full((32, 128), -4.0, F32)
+        for k in range(8):
+            line = message[24 + k : 25 + k, :]
+            first = jnp.where(which == k, line[:, :128] + part, first)
+            second = jnp.where(which == k, line[:, 128:] + part, second)
+        load = jnp.concatenate([first] * 6, axis=1) == iota((32, 768), 1).astype(F32)
+        field = jnp.concatenate([second] * 8, axis=1) == iota((32, 1024), 1).astype(F32)
+        return load.astype(F32).astype(BF16), field.astype(F32).astype(BF16)
+
+    def split(value):
         high = value.astype(BF16)
         low = (value - high.astype(F32)).astype(BF16)
+        return jnp.concatenate([high, low], axis=0)
+
+    def permuted(turn, face, rows):
         both = jnp.dot(
-            jnp.concatenate([high, low], axis=0), permute[face], preferred_element_type=F32
+            split(income[turn, face, rows, :]), permute[face], preferred_element_type=F32
         )
-        return both[:ROWS] + both[ROWS:]
-
-    def alive_of(face):
-        return live_ref[0, face].astype(F32)
+        return both[:PART] + both[PART:]
 
     def fold(value):
         return value[:, :128] + value[:, 128:]
 
-    def multiply(turn, face, rounded, matrix, field):
-        if face < 5:
-            product = jnp.dot(rounded, matrix[face], preferred_element_type=F32)
-            for n in range(6):
-                outgo[turn, n] += product[:, n * FACE : (n + 1) * FACE]
-            return None
-        total = jnp.zeros((ROWS, 128), F32)
+    def sweep(turn, half, update, matrix, field):
+        rows = rows_of(half)
+
+        def body(face, carry):
+            face_wait(face_recv, turn, half, face)
+            value = update(face, rows)
+            if matrix is not None:
+                product = jnp.dot(
+                    value.astype(BF16), matrix[face], preferred_element_type=F32
+                )
+                for n in range(6):
+                    outgo[turn, n, rows, :] += product[:, n * FACE : (n + 1) * FACE]
+            return carry
+
+        if matrix is None:
+            lax.fori_loop(0, 6, body, 0)
+            return
+        lax.fori_loop(0, 5, body, 0)
+        face_wait(face_recv, turn, half, 5)
+        rounded = update(5, rows).astype(BF16)
+        total = jnp.zeros((PART, 128), F32)
         for n in SEND_ORDER:
-            value = outgo[turn, n] + jnp.dot(
-                rounded, matrix[face, :, n * FACE : (n + 1) * FACE], preferred_element_type=F32
+            value = outgo[turn, n, rows, :] + jnp.dot(
+                rounded, matrix[5, :, n * FACE : (n + 1) * FACE], preferred_element_type=F32
             )
-            outgo[turn, n] = value
-            face_copy(turn + 1, n).start()
-            total = total + fold(field[n] * value)
-        return total
-
-    def lane_row(total):
-        return jnp.sum(total.T, axis=0, keepdims=True)
+            outgo[turn, n, rows, :] = value
+            face_copy(turn + 1, half, n).start()
+            total = total + fold(field[n, rows, :] * value)
+        dots[rows, :] = total
+
+    def both_halves(turn, update, matrix, field):
+        def body(half, carry):
+            sweep(turn, half, update, matrix, field)
+            return carry
+
+        lax.fori_loop(0, 2, body, 0)
+
+    def lane_row():
+        return jnp.sum(dots[...].T, axis=0, keepdims=True)
 
     def spread_rows(line):
         wide_ = jnp.broadcast_to(line, (128, 128)).T
@@ -282,16 +325,25 @@
         fan_wait(fan_recv, 4 + turn, s2recv.at[turn])
         return jnp.sum(s2recv[turn], axis=0)
 
-    def coarse_start(turn, terms):
+    def coarse_start(turn, source):
+        def body(face, terms):
+            return terms + lax.dot_general(
+                split(outgo[source, face]), wide[face], NT, preferred_element_type=F32
+            )
+
+        terms = lax.fori_loop(0, 6, body, jnp.zeros((2 * ROWS, 256), F32))
+        terms = terms[:ROWS] + terms[ROWS:]
         high = terms.astype(BF16)
         rest = terms - high.astype(F32)
-        middle = rest.astype(BF16)
-        low = (rest - middle.astype(F32)).astype(BF16)
-        stacked = jnp.concatenate([high, middle, low], axis=0)
-        full = jnp.dot(stacked, spread[...], preferred_element_type=F32)
-        full = full[:ROWS] + full[ROWS : 2 * ROWS] + full[2 * ROWS :]
+        stacked = jnp.concatenate([high, split(rest)], axis=0)
         for half in range(2):
-            lsend[turn, half] = full[:, half * HALF : (half + 1) * HALF].reshape(16, 8, HALF)
+            full = jnp.dot(
+                stacked,
+                spread[:, half * HALF : (half + 1) * HALF],
+                preferred_element_type=F32,
+            )
+            full = full[:ROWS] + full[ROWS : 2 * ROWS] + full[2 * ROWS :]
+            lsend[turn, half] = full.reshape(16, 8, HALF)
         fan_out(
             7 + turn,
             plane_peer,
@@ -327,6 +379,11 @@
         pieces = []
         for plane_z in range(8):
             both = crecv[turn, 2 * plane_z] + crecv[turn, 2 * plane_z + 1]
+            if turn == 0:
+                csave[plane_z] = both
+            else:
+                mine = pl.ds(pl.multiple_of(group * 8, 8), 8)
+                both = both + beta_rows[mine, :] * csave[plane_z]
             pieces.append(both[:, :128])
             energy = energy + both[:, :128] * both[:, 128:]
         energy = jnp.sum(energy, axis=1, keepdims=True)
@@ -338,42 +395,42 @@
     def coarse_values(turn):
         fan_wait(fan_recv, 13 + turn, frecv.at[turn])
         field = frecv[turn].reshape(ROWS, 1024)
-        values = lax.dot_general(
+        values[...] = lax.dot_general(
             field.astype(BF16), pick[...], NT, preferred_element_type=F32
         ).astype(BF16)
-        energy = jnp.broadcast_to(field[:, 96:97], (ROWS, FACE))
-        return values, energy
+        return jnp.broadcast_to(field[:, 96:97], (ROWS, FACE))
 
     clear(0)
+
+    def first_residual(face, rows):
+        value = alive_of(face) * loads[face, rows, :] + permuted(0, face, rows)
+        resid[face, rows, :] = value
+        return value
+
     prec_copy.wait()
-    for face in range(6):
-        face_arrived(0, face)
-        value = alive_of(face) * loads[face] + permuted(0, face)
-        resid[face] = value
-        dots = multiply(0, face, value.astype(BF16), prec, resid)
-    first_rz = lane_row(dots)
+    both_halves(0, first_residual, prec, resid)
+    first_rz = lane_row()
 
     clear(1)
     wide[...] = jnp.zeros_like(wide)
+    spread[...] = jnp.zeros_like(spread)
+    pick[...] = jnp.zeros_like(pick)
     for face in range(6):
-        wide[0:32, face * FACE : (face + 1) * FACE] = (
-            bmsg[face, :, :FACE] * alive_of(face)
+        wide[face, 0:32, :] = jnp.where(
+            iota((32, FACE), 0) < 24, bmsg[face] * alive_of(face), 0.0
         ).astype(BF16)
-    lane = iota((32, 1024), 1).astype(F32)
-    pick[...] = jnp.zeros_like(pick)
-    pick[0:32, :] = (
-        (jnp.concatenate([placed_f] * 8, axis=1) == lane).astype(F32).astype(BF16)
-    )
+    spread[0:32, :], pick[0:32, :] = one_hot(bmsg[0])
     for face in range(6):
         b_copies[SEND_ORDER.index(face ^ 1)].wait_recv()
         start = 32 * (face + 1)
-        wide[start : start + 32, face * FACE : (face + 1) * FACE] = jnp.dot(
-            brecv[face, :, :FACE].astype(BF16), permute[face], preferred_element_type=F32
+        rest = jnp.where(iota((32, FACE), 0) < 24, brecv[face], 0.0).astype(BF16)
+        wide[face, start : start + 32, :] = jnp.dot(
+            rest, permute[face], preferred_element_type=F32
         ).astype(BF16)
-        place = brecv[face, :, FACE:]
-        pick[start : start + 32, :] = (
-            (jnp.concatenate([place] * 8, axis=1) == lane).astype(F32).astype(BF16)
-        )
+        spread[start : start + 32, :], pick[start : start + 32, :] = one_hot(brecv[face])
+
+    coarse_start(0, 0)
+
     fan_wait(fan_recv, 0, kplane)
     line = iota((128, 256), 0)
     packed = third(line)
@@ -395,69 +452,74 @@
     ksel[128:256, :] = jnp.where(
         line < 96, (iota((128, HALF), 1) + HALF * core == wanted).astype(F32), 0.0
     )
-
     oper_copy.wait()
+
     rz = None
     for iteration in range(2):
         back = 2 * iteration + 1
-        terms = jnp.zeros((ROWS, 32), F32)
-        for face in range(6):
-            face_arrived(back, face)
-            value = alive_of(face) * outgo[back - 1, face] + permuted(back, face)
+        if iteration == 0:
+            coarse_sum(0)
+        else:
+            coarse_start(1, 2)
+            scalars_middle(1)
+            coarse_sum(1)
+            new_rz = scalars_end(1)[0:1]
+            beta_rows[...] = spread_rows(new_rz / rz)
+            rz = new_rz
+
+        def new_direction(face, rows):
+            value = alive_of(face) * outgo[back - 1, face, rows, :] + permuted(back, face, rows)
             if iteration == 1:
-                if face == 0:
-                    scalars_middle(1)
-                    new_rz = scalars_end(1)[0:1]
-                    beta = spread_rows(new_rz / rz)
-                    rz = new_rz
-                value = value + beta * direc[face]
-            direc[face] = value
-            rounded = value.astype(BF16)
-            terms = terms + lax.dot_general(
-                rounded,
-                own_bt[:, face * FACE : (face + 1) * FACE],
-                NT,
-                preferred_element_type=F32,
-            )
-            dots = multiply(back, face, rounded, oper, direc)
-        coarse_start(iteration, terms)
-        scalars_start(2 * iteration, lane_row(dots), first_rz)
-        coarse_sum(iteration)
+                value = value + beta_rows[rows, :] * direc[face, rows, :]
+            direc[face, rows, :] = value
+            return value
+
+        sweep(back, 0, new_direction, oper, direc)
+        coarse_apply(iteration)
+        sweep(back, 1, new_direction, oper, direc)
+        scalars_start(2 * iteration, lane_row(), first_rz)
+        coarse_share(iteration)
         scalars_middle(2 * iteration)
-        coarse_apply(iteration)
+        if iteration == 0:
+            clear(2)
+            clear(3)
+        energy = coarse_values(iteration)
         totals = scalars_end(2 * iteration)
         if iteration == 0:
             rz = totals[1:2]
-            clear(2)
-        coarse_share(iteration)
+        beta_rows[...] = spread_rows(rz) / (spread_rows(totals[0:1]) + energy)
+
+        def new_residual(face, rows):
+            cols = pl.ds(pl.multiple_of(face * FACE, FACE), FACE)
+            image = (
+                alive_of(face) * outgo[back, face, rows, :]
+                + permuted(back + 1, face, rows)
+                + jnp.dot(values[rows, :], wide[face], preferred_element_type=F32)
+            )
+            step = beta_rows[rows, :]
+            gain = step * direc[face, rows, :]
+            value = resid[face, rows, :] - step * image
+            if iteration == 0:
+                mult_out[rows, cols] = gain
+                resid[face, rows, :] = value
+            else:
+                mult_out[rows, cols] += gain
+                res_out[rows, cols] = value
+            return value
+
         if iteration == 0:
-            clear(3)
-        values, energy = coarse_values(iteration)
-        curvature = spread_rows(totals[0:1]) + energy
-        step = spread_rows(rz) / curvature
-        for face in range(6):
-            face_arrived(back + 1, face)
-            cols = slice(face * FACE, (face + 1) * FACE)
-            image = (
-                alive_of(face) * outgo[back, face]
-                + permuted(back + 1, face)
-                + jnp.dot(values, wide[:, cols], preferred_element_type=F32)
-            )
-            gain = step * direc[face]
-            value = resid[face] - step * image
-            if iteration == 0:
-                mult_out[:, cols] = gain
-                resid[face] = value
-                dots = multiply(2, face, value.astype(BF16), prec, resid)
-            else:
-                mult_out[:, cols] += gain
-                res_out[:, cols] = value
-        if iteration == 0:
-            scalars_start(1, lane_row(dots), first_rz)
-
-    for turn in range(5):
-        for face in range(6):
-            face_copy(turn, face).wait_send()
+            both_halves(2, new_residual, prec, resid)
+            scalars_start(1, lane_row(), first_rz)
+        else:
+            both_halves(4, new_residual, None, None)
+
+    def drain(index, carry):
+        half, face = index // 6, lax.rem(index, 6)
+        for turn in range(5):
+            face_wait(face_send, turn, half, face)
+        return carry
+
+    lax.fori_loop(0, 12, drain, 0)
     for copy in b_copies:
         copy.wait_send()
     fan_wait(fan_send, 0, kplane)
@@ -495,15 +557,18 @@
             buf(4, 6, ROWS, FACE),
             buf(5, 6, ROWS, FACE),
             buf(6, FACE, FACE, dtype=BF16),
-            buf(32, ORDER, dtype=BF16),
-            buf(256, ORDER, dtype=BF16),
+            buf(6, 256, FACE, dtype=BF16),
             buf(256, 1024, dtype=BF16),
-            buf(32, 768, dtype=BF16),
-            buf(6, 32, 384),
-            buf(6, 32, 384),
+            buf(256, 768, dtype=BF16),
+            buf(ROWS, 256, dtype=BF16),
+            buf(6, 32, FACE),
+            buf(6, 32, FACE),
             buf(2, 8, HALF),
             buf(32, 8, HALF),
             buf(256, HALF),
+            buf(8, 8, 256),
+            buf(ROWS, 128),
+            buf(ROWS, 256),
             buf(2, 2, 16, 8, HALF),
             buf(2, 32, 8, HALF),
             buf(2, 8, HALF),
@@ -518,8 +583,8 @@
             buf(3, 16, 8, 128),
             dma((6,)),
             dma((2,)),
-            dma((5, 6)),
-            dma((5, 6)),
+            dma((5, 2, 6)),
+            dma((5, 2, 6)),
             dma((6,)),
             dma((6,)),
             dma((15,)),
@@ -536,7 +601,7 @@
         load_terms[0],
         oper.reshape(6, FACE, ORDER),
         prec.reshape(6, FACE, ORDER),
-        coupling[0],
+        coupling[0].T,
         kinv,
         face_map.reshape(6, 1, FACE),
         face_live,

time: 188 us -> 161 us (0.86)
  Pallas kernels: 181 us -> 155 us
    pallas_call x1, Pallas kernels: 181 us -> 155 us  [local(): pl.pallas_call(kernel, out_shape=(field, field), in_specs=[any_, any_, an...]
    unnamed x3 -> x2, local copies, waits for them, and re-layouts: 5.94 us -> 4.14 us
where the time goes in v2:
time: 161 us; the launch traced here: 160 us
  Pallas kernels  155 us (96%)
  local copies, waits for them, and re-layouts  4.14 us (3%)
    pallas_call x1, Pallas kernels, local(): pl.pallas_call(kernel, out_shape=(field, field), in_specs=[any_, any_, an...  155 us
    unnamed x2, local copies, waits for them, and re-layouts  4.14 us

profile of v2, /device:TPU:1, one launch (start us, length us, event | category | flops | bytes accessed | tf_op | source)
XLA Modules:
  0.0 159.5 jit_solution(17862111792639875659)
XLA Ops:
  0.6 154.7 %feti_solve.1 = (f32[128,1536]{1,0:T(8,128)}, f32[128,1536]{1,0:T(8,128)}) custom-call(f32[128,1536]{1,0:T(8,128)} %bitcast.11, bf16[6,256,1536]{2,1,0:T(8,128)(2,1)} %bitcast.9, bf16[6,256,1536]{2,1,0:T(8,128)(2,1)} %bitcast.10, bf16[24,1536]{1,0:T(8,128)(2,1)} %bitcast.14, f32[3,768]{1,0:T(4,128)} %kinv_ref.1, s32[6,1,256]{2,1,0:T(1,128)} %bitcast.15, ...), custom_call_target="tpu_custom_call" | custom-call | flops 2600000000 | bytes 12000000 | tf_op jit(solution)/shard_map/feti_solve/pallas_call | solution.py:546
  155.4 2.1 %copy.12 = f32[1,128,1536]{2,1,0:T(8,128)} copy(f32[1,128,1536]{2,1,0:T(8,128)} %bitcast.13) | data formatting | bytes 1572864
  157.4 2.1 %copy.13 = f32[1,128,1536]{2,1,0:T(8,128)} copy(f32[1,128,1536]{2,1,0:T(8,128)} %bitcast.12) | data formatting | bytes 1572864

commit v3 on v2

--- a/solution.py
+++ b/solution.py
@@ -57,7 +57,10 @@
     ksel,
     csave,
     dots,
+    step_rows,
     beta_rows,
+    zed,
+    qdir,
     lsend,
     lrecv,
     zsend,
@@ -178,11 +181,9 @@
 
     pl.semaphore_wait(barrier, 6 + 31 + 15)
 
-    for half in range(2):
-        for face in SEND_ORDER:
-            if half == 0:
-                load_copies[face].wait()
-            face_copy(0, half, face).start()
+    for face in SEND_ORDER:
+        load_copies[face].wait()
+        face_copy(0, 0, face).start()
 
     turned = coup_ref[...].astype(F32)
     zero = jnp.zeros((8, FACE), F32)
@@ -212,6 +213,8 @@
         )
         copy.start()
         b_copies.append(copy)
+    for face in SEND_ORDER:
+        face_copy(0, 1, face).start()
 
     kown[...] = jnp.zeros_like(kown)
     kown[0, 0:3, :] = kinv_ref[:, :HALF]
@@ -230,12 +233,12 @@
 
     lax.fori_loop(0, 6, build_permute, 0)
 
-    def clear(turn):
-        def body(face, carry):
+    def clear(face, carry):
+        for turn in range(4):
             outgo[turn, face] = jnp.zeros((ROWS, FACE), F32)
-            return carry
-
-        lax.fori_loop(0, 6, body, 0)
+        return carry
+
+    lax.fori_loop(0, 6, clear, 0)
 
     row = iota((32, 128), 0)
     which = third(row)
@@ -266,8 +269,8 @@
     def fold(value):
         return value[:, :128] + value[:, 128:]
 
-    def sweep(turn, half, update, matrix, field):
-        rows = rows_of(half)
+    def sweep(turn, half, update, matrix, products):
+        rows = slice(half * PART, (half + 1) * PART)
 
         def body(face, carry):
             face_wait(face_recv, turn, half, face)
@@ -286,44 +289,43 @@
         lax.fori_loop(0, 5, body, 0)
         face_wait(face_recv, turn, half, 5)
         rounded = update(5, rows).astype(BF16)
-        total = jnp.zeros((PART, 128), F32)
+        totals = [jnp.zeros((PART, 128), F32)] * len(products)
         for n in SEND_ORDER:
             value = outgo[turn, n, rows, :] + jnp.dot(
                 rounded, matrix[5, :, n * FACE : (n + 1) * FACE], preferred_element_type=F32
             )
             outgo[turn, n, rows, :] = value
             face_copy(turn + 1, half, n).start()
-            total = total + fold(field[n, rows, :] * value)
-        dots[rows, :] = total
-
-    def both_halves(turn, update, matrix, field):
-        def body(half, carry):
-            sweep(turn, half, update, matrix, field)
-            return carry
-
-        lax.fori_loop(0, 2, body, 0)
-
-    def lane_row():
-        return jnp.sum(dots[...].T, axis=0, keepdims=True)
+            totals = [
+                total + fold(make(n, rows, value))
+                for total, (_, make) in zip(totals, products)
+            ]
+        for total, (place, _) in zip(totals, products):
+            dots[place, rows, :] = total
+
+    def lane_row(place):
+        return jnp.sum(dots[place].T, axis=0, keepdims=True)
 
     def spread_rows(line):
         wide_ = jnp.broadcast_to(line, (128, 128)).T
         return jnp.concatenate([wide_, wide_], axis=1)
 
-    def scalars_start(turn, first, second):
-        s1send[turn] = jnp.concatenate([first, second, jnp.zeros((6, 128), F32)], axis=0)
-        fan_out(1 + turn, group_peer, 16, group, lambda q: s1send.at[turn], s1recv.at[turn])
-        s1recv[turn, group] = s1send[turn]
-
-    def scalars_middle(turn):
-        fan_wait(fan_recv, 1 + turn, s1recv.at[turn])
-        s2send[turn] = jnp.sum(s1recv[turn], axis=0)
-        fan_out(4 + turn, column_peer, 16, column, lambda q: s2send.at[turn], s2recv.at[turn])
-        s2recv[turn, column] = s2send[turn]
-
-    def scalars_end(turn):
-        fan_wait(fan_recv, 4 + turn, s2recv.at[turn])
-        return jnp.sum(s2recv[turn], axis=0)
+    def scalars_start(slot, places):
+        lines = [lane_row(place) for place in places]
+        lines.append(jnp.zeros((8 - len(places), 128), F32))
+        s1send[slot] = jnp.concatenate(lines, axis=0)
+        fan_out(1 + slot, group_peer, 16, group, lambda q: s1send.at[slot], s1recv.at[slot])
+        s1recv[slot, group] = s1send[slot]
+
+    def scalars_middle(slot):
+        fan_wait(fan_recv, 1 + slot, s1recv.at[slot])
+        s2send[slot] = jnp.sum(s1recv[slot], axis=0)
+        fan_out(5 + slot, column_peer, 16, column, lambda q: s2send.at[slot], s2recv.at[slot])
+        s2recv[slot, column] = s2send[slot]
+
+    def scalars_end(slot):
+        fan_wait(fan_recv, 5 + slot, s2recv.at[slot])
+        return jnp.sum(s2recv[slot], axis=0)
 
     def coarse_start(turn, source):
         def body(face, terms):
@@ -345,7 +347,7 @@
             full = full[:ROWS] + full[ROWS : 2 * ROWS] + full[2 * ROWS :]
             lsend[turn, half] = full.reshape(16, 8, HALF)
         fan_out(
-            7 + turn,
+            9 + turn,
             plane_peer,
             32,
             plane,
@@ -355,13 +357,13 @@
         lrecv[turn, plane] = lsend[turn, core, group]
 
     def coarse_sum(turn):
-        fan_wait(fan_recv, 7 + turn, lrecv.at[turn])
+        fan_wait(fan_recv, 9 + turn, lrecv.at[turn])
         zsend[turn] = jnp.sum(lrecv[turn], axis=0)
-        fan_out(9 + turn, z_peer, 8, z, lambda q: zsend.at[turn], zrecv.at[turn])
+        fan_out(11 + turn, z_peer, 8, z, lambda q: zsend.at[turn], zrecv.at[turn])
         zrecv[turn, z] = zsend[turn]
 
     def coarse_apply(turn):
-        fan_wait(fan_recv, 9 + turn, zrecv.at[turn])
+        fan_wait(fan_recv, 11 + turn, zrecv.at[turn])
         load = jnp.sum(zrecv[turn], axis=0)
         csend[turn] = lax.dot_general(
             load,
@@ -370,48 +372,100 @@
             precision=lax.Precision.HIGHEST,
             preferred_element_type=F32,
         )
-        fan_out(11 + turn, column_peer, 16, column, lambda q: csend.at[turn], crecv.at[turn])
+        fan_out(13 + turn, column_peer, 16, column, lambda q: csend.at[turn], crecv.at[turn])
         crecv[turn, column] = csend[turn]
 
     def coarse_share(turn):
-        fan_wait(fan_recv, 11 + turn, crecv.at[turn])
+        fan_wait(fan_recv, 13 + turn, crecv.at[turn])
         energy = jnp.zeros((8, 128), F32)
+        cross = jnp.zeros((8, 128), F32)
         pieces = []
         for plane_z in range(8):
             both = crecv[turn, 2 * plane_z] + crecv[turn, 2 * plane_z + 1]
+            field, load = both[:, :128], both[:, 128:]
             if turn == 0:
                 csave[plane_z] = both
             else:
-                mine = pl.ds(pl.multiple_of(group * 8, 8), 8)
-                both = both + beta_rows[mine, :] * csave[plane_z]
-            pieces.append(both[:, :128])
-            energy = energy + both[:, :128] * both[:, 128:]
+                saved = csave[plane_z]
+                cross = cross + field * saved[:, 128:] + saved[:, :128] * load
+            pieces.append(field)
+            energy = energy + field * load
+        lane = iota((8, 128), 1)
         energy = jnp.sum(energy, axis=1, keepdims=True)
-        pieces[0] = jnp.where(iota((8, 128), 1) == 96, energy, pieces[0])
+        pieces[0] = jnp.where(lane == 96, energy, pieces[0])
+        if turn == 1:
+            cross = jnp.sum(cross, axis=1, keepdims=True)
+            pieces[0] = jnp.where(lane == 97, cross, pieces[0])
         fsend[turn] = jnp.concatenate(pieces, axis=1)
-        fan_out(13 + turn, group_peer, 16, group, lambda q: fsend.at[turn], frecv.at[turn])
+        fan_out(15 + turn, group_peer, 16, group, lambda q: fsend.at[turn], frecv.at[turn])
         frecv[turn, group] = fsend[turn]
 
-    def coarse_values(turn):
-        fan_wait(fan_recv, 13 + turn, frecv.at[turn])
-        field = frecv[turn].reshape(ROWS, 1024)
-        values[...] = lax.dot_general(
+    def coarse_values(turn, half):
+        rows = slice(half * PART, (half + 1) * PART)
+        field = frecv[turn, 8 * half : 8 * half + 8].reshape(PART, 1024)
+        energy = field[:, 96:97]
+        if turn == 1:
+            before = frecv[0, 8 * half : 8 * half + 8].reshape(PART, 1024)
+            beta = beta_rows[rows, :]
+            energy = energy + beta[:, 0:1] * (
+                field[:, 97:98] + beta[:, 0:1] * before[:, 96:97]
+            )
+            field = field + jnp.concatenate([beta] * 4, axis=1) * before
+        values[rows, :] = lax.dot_general(
             field.astype(BF16), pick[...], NT, preferred_element_type=F32
         ).astype(BF16)
-        return jnp.broadcast_to(field[:, 96:97], (ROWS, FACE))
-
-    clear(0)
+        return jnp.broadcast_to(energy, (PART, FACE))
 
     def first_residual(face, rows):
         value = alive_of(face) * loads[face, rows, :] + permuted(0, face, rows)
         resid[face, rows, :] = value
         return value
 
+    def first_direction(face, rows):
+        value = alive_of(face) * outgo[0, face, rows, :] + permuted(1, face, rows)
+        direc[face, rows, :] = value
+        return value
+
+    def second_residual(face, rows):
+        cols = pl.ds(pl.multiple_of(face * FACE, FACE), FACE)
+        direct = alive_of(face) * outgo[1, face, rows, :] + permuted(2, face, rows)
+        qdir[face, rows, :] = direct
+        image = direct + jnp.dot(values[rows, :], wide[face], preferred_element_type=F32)
+        step = step_rows[rows, :]
+        mult_out[rows, cols] = step * direc[face, rows, :]
+        value = resid[face, rows, :] - step * image
+        resid[face, rows, :] = value
+        return value
+
+    def second_precond(face, rows):
+        value = alive_of(face) * outgo[2, face, rows, :] + permuted(3, face, rows)
+        zed[face, rows, :] = value
+        return value
+
+    def last_residual(face, rows):
+        cols = pl.ds(pl.multiple_of(face * FACE, FACE), FACE)
+        step, beta = step_rows[rows, :], beta_rows[rows, :]
+        image = (
+            alive_of(face) * outgo[3, face, rows, :]
+            + permuted(4, face, rows)
+            + beta * qdir[face, rows, :]
+            + jnp.dot(values[rows, :], wide[face], preferred_element_type=F32)
+        )
+        mult_out[rows, cols] += step * (zed[face, rows, :] + beta * direc[face, rows, :])
+        res_out[rows, cols] = resid[face, rows, :] - step * image
+
+    with_residual = lambda n, rows, value: resid[n, rows, :] * value
+    with_direction = lambda n, rows, value: direc[n, rows, :] * value
+    with_precond = lambda n, rows, value: zed[n, rows, :] * value
+    crossed = (
+        lambda n, rows, value: zed[n, rows, :] * outgo[1, n, rows, :]
+        + direc[n, rows, :] * value
+    )
+
+    dots[...] = jnp.zeros_like(dots)
     prec_copy.wait()
-    both_halves(0, first_residual, prec, resid)
-    first_rz = lane_row()
-
-    clear(1)
+    sweep(0, 0, first_residual, prec, [(0, with_residual)])
+
     wide[...] = jnp.zeros_like(wide)
     spread[...] = jnp.zeros_like(spread)
     pick[...] = jnp.zeros_like(pick)
@@ -429,8 +483,6 @@
         ).astype(BF16)
         spread[start : start + 32, :], pick[start : start + 32, :] = one_hot(brecv[face])
 
-    coarse_start(0, 0)
-
     fan_wait(fan_recv, 0, kplane)
     line = iota((128, 256), 0)
     packed = third(line)
@@ -452,66 +504,56 @@
     ksel[128:256, :] = jnp.where(
         line < 96, (iota((128, HALF), 1) + HALF * core == wanted).astype(F32), 0.0
     )
+    sweep(0, 1, first_residual, prec, [(0, with_residual)])
+    coarse_start(0, 0)
     oper_copy.wait()
-
-    rz = None
-    for iteration in range(2):
-        back = 2 * iteration + 1
-        if iteration == 0:
-            coarse_sum(0)
-        else:
-            coarse_start(1, 2)
+    coarse_sum(0)
+    sweep(1, 0, first_direction, oper, [(1, with_direction)])
+    scalars_start(0, (0, 1))
+    coarse_apply(0)
+    scalars_middle(0)
+    sweep(1, 1, first_direction, oper, [(1, with_direction)])
+    scalars_start(1, (0, 1))
+    coarse_share(0)
+
+    saved = []
+    fan_wait(fan_recv, 15, frecv.at[0])
+    for half in range(2):
+        rows = slice(half * PART, (half + 1) * PART)
+        totals = scalars_end(half)
+        saved.append(totals)
+        energy = coarse_values(0, half)
+        step_rows[rows, :] = spread_rows(totals[0:1])[rows] / (
+            spread_rows(totals[1:2])[rows] + energy
+        )
+        if half == 0:
             scalars_middle(1)
-            coarse_sum(1)
-            new_rz = scalars_end(1)[0:1]
-            beta_rows[...] = spread_rows(new_rz / rz)
-            rz = new_rz
-
-        def new_direction(face, rows):
-            value = alive_of(face) * outgo[back - 1, face, rows, :] + permuted(back, face, rows)
-            if iteration == 1:
-                value = value + beta_rows[rows, :] * direc[face, rows, :]
-            direc[face, rows, :] = value
-            return value
-
-        sweep(back, 0, new_direction, oper, direc)
-        coarse_apply(iteration)
-        sweep(back, 1, new_direction, oper, direc)
-        scalars_start(2 * iteration, lane_row(), first_rz)
-        coarse_share(iteration)
-        scalars_middle(2 * iteration)
-        if iteration == 0:
-            clear(2)
-            clear(3)
-        energy = coarse_values(iteration)
-        totals = scalars_end(2 * iteration)
-        if iteration == 0:
-            rz = totals[1:2]
-        beta_rows[...] = spread_rows(rz) / (spread_rows(totals[0:1]) + energy)
-
-        def new_residual(face, rows):
-            cols = pl.ds(pl.multiple_of(face * FACE, FACE), FACE)
-            image = (
-                alive_of(face) * outgo[back, face, rows, :]
-                + permuted(back + 1, face, rows)
-                + jnp.dot(values[rows, :], wide[face], preferred_element_type=F32)
-            )
-            step = beta_rows[rows, :]
-            gain = step * direc[face, rows, :]
-            value = resid[face, rows, :] - step * image
-            if iteration == 0:
-                mult_out[rows, cols] = gain
-                resid[face, rows, :] = value
-            else:
-                mult_out[rows, cols] += gain
-                res_out[rows, cols] = value
-            return value
-
-        if iteration == 0:
-            both_halves(2, new_residual, prec, resid)
-            scalars_start(1, lane_row(), first_rz)
-        else:
-            both_halves(4, new_residual, None, None)
+        sweep(2, half, second_residual, prec, [(2, with_residual)])
+    coarse_start(1, 2)
+    coarse_sum(1)
+    second = [(3, with_precond), (4, crossed)]
+    sweep(3, 0, second_precond, oper, second)
+    scalars_start(2, (2, 3, 4))
+    coarse_apply(1)
+    scalars_middle(2)
+    sweep(3, 1, second_precond, oper, second)
+    scalars_start(3, (2, 3, 4))
+    coarse_share(1)
+
+    fan_wait(fan_recv, 16, frecv.at[1])
+    for half in range(2):
+        rows = slice(half * PART, (half + 1) * PART)
+        totals = scalars_end(2 + half)
+        beta_line = totals[0:1] / saved[half][0:1]
+        beta_rows[rows, :] = spread_rows(beta_line)[rows]
+        curvature = totals[1:2] + beta_line * (totals[2:3] + beta_line * saved[half][1:2])
+        energy = coarse_values(1, half)
+        step_rows[rows, :] = spread_rows(totals[0:1])[rows] / (
+            spread_rows(curvature)[rows] + energy
+        )
+        if half == 0:
+            scalars_middle(3)
+        sweep(4, half, last_residual, None, None)
 
     def drain(index, carry):
         half, face = index // 6, lax.rem(index, 6)
@@ -523,14 +565,14 @@
     for copy in b_copies:
         copy.wait_send()
     fan_wait(fan_send, 0, kplane)
-    for turn in range(3):
-        fan_wait(fan_send, 1 + turn, s1recv.at[turn])
-        fan_wait(fan_send, 4 + turn, s2recv.at[turn])
+    for slot in range(4):
+        fan_wait(fan_send, 1 + slot, s1recv.at[slot])
+        fan_wait(fan_send, 5 + slot, s2recv.at[slot])
     for turn in range(2):
-        fan_wait(fan_send, 7 + turn, lrecv.at[turn])
-        fan_wait(fan_send, 9 + turn, zrecv.at[turn])
-        fan_wait(fan_send, 11 + turn, crecv.at[turn])
-        fan_wait(fan_send, 13 + turn, frecv.at[turn])
+        fan_wait(fan_send, 9 + turn, lrecv.at[turn])
+        fan_wait(fan_send, 11 + turn, zrecv.at[turn])
+        fan_wait(fan_send, 13 + turn, crecv.at[turn])
+        fan_wait(fan_send, 15 + turn, frecv.at[turn])
 
 
 def local(load_terms, oper, prec, coupling, kinv, face_map, face_live, ids):
@@ -567,8 +609,11 @@
             buf(32, 8, HALF),
             buf(256, HALF),
             buf(8, 8, 256),
-            buf(ROWS, 128),
-            buf(ROWS, 256),
+            buf(5, ROWS, 128),
+            buf(ROWS, FACE),
+            buf(ROWS, FACE),
+            buf(6, ROWS, FACE),
+            buf(6, ROWS, FACE),
             buf(2, 2, 16, 8, HALF),
             buf(2, 32, 8, HALF),
             buf(2, 8, HALF),
@@ -577,18 +622,18 @@
             buf(2, 16, 8, 256),
             buf(2, 8, 1024),
             buf(2, 16, 8, 1024),
-            buf(3, 8, 128),
-            buf(3, 16, 8, 128),
-            buf(3, 8, 128),
-            buf(3, 16, 8, 128),
+            buf(4, 8, 128),
+            buf(4, 16, 8, 128),
+            buf(4, 8, 128),
+            buf(4, 16, 8, 128),
             dma((6,)),
             dma((2,)),
             dma((5, 2, 6)),
             dma((5, 2, 6)),
             dma((6,)),
             dma((6,)),
-            dma((15,)),
-            dma((15,)),
+            dma((17,)),
+            dma((17,)),
         ],
         compiler_params=pltpu.CompilerParams(
             collective_id=0, has_side_effects=True, vmem_limit_bytes=60 * 1024 * 1024

time: 161 us -> 159 us (0.988); the launches traced: 160 us -> 159 us
  no operation moved by 1% of the time
where the time goes in v3:
time: 159 us
  Pallas kernels  155 us (97%)
  local copies, waits for them, and re-layouts  4.14 us (3%)
    pallas_call x1, Pallas kernels, local(): pl.pallas_call(kernel, out_shape=(field, field), in_specs=[any_, any_, an...  155 us
    unnamed x2, local copies, waits for them, and re-layouts  4.14 us

profile of v3, /device:TPU:1, one launch (start us, length us, event | category | flops | bytes accessed | tf_op | source)
XLA Modules:
  0.0 159.3 jit_solution(9682453509815568831)
XLA Ops:
  0.6 154.5 %feti_solve.1 = (f32[128,1536]{1,0:T(8,128)}, f32[128,1536]{1,0:T(8,128)}) custom-call(f32[128,1536]{1,0:T(8,128)} %bitcast.11, bf16[6,256,1536]{2,1,0:T(8,128)(2,1)} %bitcast.9, bf16[6,256,1536]{2,1,0:T(8,128)(2,1)} %bitcast.10, bf16[24,1536]{1,0:T(8,128)(2,1)} %bitcast.14, f32[3,768]{1,0:T(4,128)} %kinv_ref.1, s32[6,1,256]{2,1,0:T(1,128)} %bitcast.15, ...), custom_call_target="tpu_custom_call" | custom-call | flops 2600000000 | bytes 12000000 | tf_op jit(solution)/shard_map/feti_solve/pallas_call | solution.py:588
  155.2 2.1 %copy.12 = f32[1,128,1536]{2,1,0:T(8,128)} copy(f32[1,128,1536]{2,1,0:T(8,128)} %bitcast.13) | data formatting | bytes 1572864
  157.2 2.1 %copy.13 = f32[1,128,1536]{2,1,0:T(8,128)} copy(f32[1,128,1536]{2,1,0:T(8,128)} %bitcast.12) | data formatting | bytes 1572864

commit v4 on v3

--- a/solution.py
+++ b/solution.py
@@ -90,6 +90,7 @@
     group = x * 4 + y
     plane = group * 2 + core
     column = z * 2 + core
+    side = x // 2
 
     def at(px, py, pz, pcore):
         return (px * 2 + pz % 2, py * 8 + (pz // 2) * 2 + pcore)
@@ -327,34 +328,54 @@
         fan_wait(fan_recv, 5 + slot, s2recv.at[slot])
         return jnp.sum(s2recv[slot], axis=0)
 
-    def coarse_start(turn, source):
+    def on_side(half, step, turn):
+        @pl.when(side == half)
+        def _():
+            step(turn)
+
+    def coarse_start(turn, half, source):
+        rows = slice(half * PART, (half + 1) * PART)
+
         def body(face, terms):
             return terms + lax.dot_general(
-                split(outgo[source, face]), wide[face], NT, preferred_element_type=F32
+                split(outgo[source, face, rows, :]), wide[face], NT, preferred_element_type=F32
             )
 
-        terms = lax.fori_loop(0, 6, body, jnp.zeros((2 * ROWS, 256), F32))
-        terms = terms[:ROWS] + terms[ROWS:]
+        terms = lax.fori_loop(0, 6, body, jnp.zeros((2 * PART, 256), F32))
+        terms = terms[:PART] + terms[PART:]
         high = terms.astype(BF16)
         rest = terms - high.astype(F32)
         stacked = jnp.concatenate([high, split(rest)], axis=0)
-        for half in range(2):
+        for part in range(2):
             full = jnp.dot(
                 stacked,
-                spread[:, half * HALF : (half + 1) * HALF],
+                spread[:, part * HALF : (part + 1) * HALF],
                 preferred_element_type=F32,
             )
-            full = full[:ROWS] + full[ROWS : 2 * ROWS] + full[2 * ROWS :]
-            lsend[turn, half] = full.reshape(16, 8, HALF)
-        fan_out(
-            9 + turn,
-            plane_peer,
-            32,
-            plane,
-            lambda q: lsend.at[turn, q % 2, q // 2],
-            lrecv.at[turn],
-        )
-        lrecv[turn, plane] = lsend[turn, core, group]
+            full = full[:PART] + full[PART : 2 * PART] + full[2 * PART :]
+            lsend[turn, part, 8 * half : 8 * half + 8] = full.reshape(8, 8, HALF)
+
+        def send(k, carry):
+            q = 16 * half + lax.rem(plane + k, 16)
+
+            @pl.when(q != plane)
+            def _():
+                pltpu.make_async_remote_copy(
+                    src_ref=lsend.at[turn, q % 2, q // 2],
+                    dst_ref=lrecv.at[turn, plane],
+                    send_sem=fan_send.at[9 + turn],
+                    recv_sem=fan_recv.at[9 + turn],
+                    device_id=plane_peer(q),
+                    device_id_type=MESH,
+                ).start()
+
+            return carry
+
+        lax.fori_loop(0, 16, send, 0)
+
+        @pl.when(side == half)
+        def _():
+            lrecv[turn, plane] = lsend[turn, core, group]
 
     def coarse_sum(turn):
         fan_wait(fan_recv, 9 + turn, lrecv.at[turn])
@@ -397,8 +418,34 @@
             cross = jnp.sum(cross, axis=1, keepdims=True)
             pieces[0] = jnp.where(lane == 97, cross, pieces[0])
         fsend[turn] = jnp.concatenate(pieces, axis=1)
-        fan_out(15 + turn, group_peer, 16, group, lambda q: fsend.at[turn], frecv.at[turn])
         frecv[turn, group] = fsend[turn]
+
+        def send(k, carry):
+            q = lax.rem(group + k, 16)
+            pltpu.make_async_remote_copy(
+                src_ref=fsend.at[turn],
+                dst_ref=frecv.at[turn, group],
+                send_sem=fan_send.at[15 + turn],
+                recv_sem=fan_recv.at[15 + turn + 2 * side],
+                device_id=group_peer(q),
+                device_id_type=MESH,
+            ).start()
+            return carry
+
+        lax.fori_loop(1, 16, send, 0)
+
+    def coarse_arrived(turn, half):
+        def wait(count):
+            part = frecv.at[turn, pl.ds(8 * half, count)]
+            pltpu.make_async_copy(part, part, fan_recv.at[15 + turn + 2 * half]).wait()
+
+        @pl.when(side == half)
+        def _():
+            wait(7)
+
+        @pl.when(side != half)
+        def _():
+            wait(8)
 
     def coarse_values(turn, half):
         rows = slice(half * PART, (half + 1) * PART)
@@ -504,24 +551,28 @@
     ksel[128:256, :] = jnp.where(
         line < 96, (iota((128, HALF), 1) + HALF * core == wanted).astype(F32), 0.0
     )
+    coarse_start(0, 0, 0)
     sweep(0, 1, first_residual, prec, [(0, with_residual)])
-    coarse_start(0, 0)
+    coarse_start(0, 1, 0)
     oper_copy.wait()
-    coarse_sum(0)
+    on_side(0, coarse_sum, 0)
+    on_side(0, coarse_apply, 0)
     sweep(1, 0, first_direction, oper, [(1, with_direction)])
     scalars_start(0, (0, 1))
-    coarse_apply(0)
+    on_side(1, coarse_sum, 0)
+    on_side(0, coarse_share, 0)
+    on_side(1, coarse_apply, 0)
     scalars_middle(0)
     sweep(1, 1, first_direction, oper, [(1, with_direction)])
     scalars_start(1, (0, 1))
-    coarse_share(0)
+    on_side(1, coarse_share, 0)
 
     saved = []
-    fan_wait(fan_recv, 15, frecv.at[0])
     for half in range(2):
         rows = slice(half * PART, (half + 1) * PART)
         totals = scalars_end(half)
         saved.append(totals)
+        coarse_arrived(0, half)
         energy = coarse_values(0, half)
         step_rows[rows, :] = spread_rows(totals[0:1])[rows] / (
             spread_rows(totals[1:2])[rows] + energy
@@ -529,24 +580,27 @@
         if half == 0:
             scalars_middle(1)
         sweep(2, half, second_residual, prec, [(2, with_residual)])
-    coarse_start(1, 2)
-    coarse_sum(1)
+        coarse_start(1, half, 2)
     second = [(3, with_precond), (4, crossed)]
+    on_side(0, coarse_sum, 1)
+    on_side(0, coarse_apply, 1)
     sweep(3, 0, second_precond, oper, second)
     scalars_start(2, (2, 3, 4))
-    coarse_apply(1)
+    on_side(1, coarse_sum, 1)
+    on_side(0, coarse_share, 1)
+    on_side(1, coarse_apply, 1)
     scalars_middle(2)
     sweep(3, 1, second_precond, oper, second)
     scalars_start(3, (2, 3, 4))
-    coarse_share(1)
-
-    fan_wait(fan_recv, 16, frecv.at[1])
+    on_side(1, coarse_share, 1)
+
     for half in range(2):
         rows = slice(half * PART, (half + 1) * PART)
         totals = scalars_end(2 + half)
         beta_line = totals[0:1] / saved[half][0:1]
         beta_rows[rows, :] = spread_rows(beta_line)[rows]
         curvature = totals[1:2] + beta_line * (totals[2:3] + beta_line * saved[half][1:2])
+        coarse_arrived(1, half)
         energy = coarse_values(1, half)
         step_rows[rows, :] = spread_rows(totals[0:1])[rows] / (
             spread_rows(curvature)[rows] + energy
@@ -632,8 +686,8 @@
             dma((5, 2, 6)),
             dma((6,)),
             dma((6,)),
-            dma((17,)),
-            dma((17,)),
+            dma((19,)),
+            dma((19,)),
         ],
         compiler_params=pltpu.CompilerParams(
             collective_id=0, has_side_effects=True, vmem_limit_bytes=60 * 1024 * 1024

time: 159 us -> 152 us (0.956)
  Pallas kernels: 155 us -> 147 us
    pallas_call x1, Pallas kernels: 155 us -> 147 us  [local(): pl.pallas_call(kernel, out_shape=(field, field), in_specs=[any_, any_, an...]
where the time goes in v4:
time: 152 us
  Pallas kernels  147 us (97%)
  local copies, waits for them, and re-layouts  4.14 us (3%)
    pallas_call x1, Pallas kernels, local(): pl.pallas_call(kernel, out_shape=(field, field), in_specs=[any_, any_, an...  147 us
    unnamed x2, local copies, waits for them, and re-layouts  4.14 us

profile of v4, /device:TPU:1, one launch (start us, length us, event | category | flops | bytes accessed | tf_op | source)
XLA Modules:
  0.0 151.8 jit_solution(11418687160042208969)
XLA Ops:
  0.6 147.0 %feti_solve.1 = (f32[128,1536]{1,0:T(8,128)}, f32[128,1536]{1,0:T(8,128)}) custom-call(f32[128,1536]{1,0:T(8,128)} %bitcast.11, bf16[6,256,1536]{2,1,0:T(8,128)(2,1)} %bitcast.9, bf16[6,256,1536]{2,1,0:T(8,128)(2,1)} %bitcast.10, bf16[24,1536]{1,0:T(8,128)(2,1)} %bitcast.14, f32[3,768]{1,0:T(4,128)} %kinv_ref.1, s32[6,1,256]{2,1,0:T(1,128)} %bitcast.15, ...), custom_call_target="tpu_custom_call" | custom-call | flops 2600000000 | bytes 12000000 | tf_op jit(solution)/shard_map/feti_solve/pallas_call | solution.py:642
  147.6 2.1 %copy.12 = f32[1,128,1536]{2,1,0:T(8,128)} copy(f32[1,128,1536]{2,1,0:T(8,128)} %bitcast.13) | data formatting | bytes 1572864
  149.7 2.1 %copy.13 = f32[1,128,1536]{2,1,0:T(8,128)} copy(f32[1,128,1536]{2,1,0:T(8,128)} %bitcast.12) | data formatting | bytes 1572864

commit v5 on v4

--- a/solution.py
+++ b/solution.py
@@ -313,7 +313,7 @@
 
     def scalars_start(slot, places):
         lines = [lane_row(place) for place in places]
-        lines.append(jnp.zeros((8 - len(places), 128), F32))
+        lines.append(jnp.zeros((4 - len(places), 128), F32))
         s1send[slot] = jnp.concatenate(lines, axis=0)
         fan_out(1 + slot, group_peer, 16, group, lambda q: s1send.at[slot], s1recv.at[slot])
         s1recv[slot, group] = s1send[slot]
@@ -676,10 +676,10 @@
             buf(2, 16, 8, 256),
             buf(2, 8, 1024),
             buf(2, 16, 8, 1024),
-            buf(4, 8, 128),
-            buf(4, 16, 8, 128),
-            buf(4, 8, 128),
-            buf(4, 16, 8, 128),
+            buf(4, 4, 128),
+            buf(4, 16, 4, 128),
+            buf(4, 4, 128),
+            buf(4, 16, 4, 128),
             dma((6,)),
             dma((2,)),
             dma((5, 2, 6)),

time: 152 us -> 150 us (0.987)
  Pallas kernels: 147 us -> 145 us
    pallas_call x1, Pallas kernels: 147 us -> 145 us  [local(): pl.pallas_call(kernel, out_shape=(field, field), in_specs=[any_, any_, an...]
where the time goes in v5:
time: 150 us
  Pallas kernels  145 us (97%)
  local copies, waits for them, and re-layouts  4.14 us (3%)
    pallas_call x1, Pallas kernels, local(): pl.pallas_call(kernel, out_shape=(field, field), in_specs=[any_, any_, an...  145 us
    unnamed x2, local copies, waits for them, and re-layouts  4.14 us

profile of v5, /device:TPU:1, one launch (start us, length us, event | category | flops | bytes accessed | tf_op | source)
XLA Modules:
  0.0 149.7 jit_solution(7258010853049616055)
XLA Ops:
  0.6 144.9 %feti_solve.1 = (f32[128,1536]{1,0:T(8,128)}, f32[128,1536]{1,0:T(8,128)}) custom-call(f32[128,1536]{1,0:T(8,128)} %bitcast.11, bf16[6,256,1536]{2,1,0:T(8,128)(2,1)} %bitcast.9, bf16[6,256,1536]{2,1,0:T(8,128)(2,1)} %bitcast.10, bf16[24,1536]{1,0:T(8,128)(2,1)} %bitcast.14, f32[3,768]{1,0:T(4,128)} %kinv_ref.1, s32[6,1,256]{2,1,0:T(1,128)} %bitcast.15, ...), custom_call_target="tpu_custom_call" | custom-call | flops 2600000000 | bytes 12000000 | tf_op jit(solution)/shard_map/feti_solve/pallas_call | solution.py:642
  145.6 2.1 %copy.12 = f32[1,128,1536]{2,1,0:T(8,128)} copy(f32[1,128,1536]{2,1,0:T(8,128)} %bitcast.13) | data formatting | bytes 1572864
  147.6 2.1 %copy.13 = f32[1,128,1536]{2,1,0:T(8,128)} copy(f32[1,128,1536]{2,1,0:T(8,128)} %bitcast.12) | data formatting | bytes 1572864
